TPU v7x, 128 devices: a whole 4x4x4 slice. The times are simulated.
128 devices in a mesh: group: 4 (over y), col: 32 (over z, x, core).
Axes of the slice: x: 4, y: 4, z: 4, core: 2. Of those that a mesh axis runs over, the one named last changes fastest.
Arguments:
- layer_input: bfloat16 [16384, 4096], P(('group', 'col')), may hold values from -6 to 6
- norm_gain: bfloat16 [4096], replicated, may hold values from 0.099609375 to 1.8984375
- keyvalue_cotangent: bfloat16 [16384, 2048], P(('group', 'col')), may hold values from -6 to 6
- keyvalue_weight: bfloat16 [4096, 2048], P('col'), may hold values from -0.125 to 0.125
- residual_cotangent: bfloat16 [16384, 4096], P(('group', 'col')), may hold values from -6 to 6
- ngram_ids: int32 [16384, 2], P(('group', 'col')), may hold values from 0 to 32767, as said below
- table: float32 [32768, 4096], P('group', 'col'), may hold values from -6 to 6
- accumulator: float32 [32768], P('group'), may hold values from 0.05 to 2
Outputs:
- new_table: float32 [32768, 4096], P('group', 'col')
- new_accum: float32 [32768], P('group')
Inputs may be any that keep to these rules, and one draw needn't show every extreme that they name: `ngram_ids`: row r belongs to owner group r // 8192. Among the 256 entries of one device's tokens (aligned blocks of 128 tokens), at most 128 belong to any one owner group, and one owner group, the same for every device, holds exactly 128 of them.
All inputs are finite; a program needn't handle non-finite values.
Results may differ from a plain program's by a relative error of at most 0.0009.
Values may be sent and summed in bfloat16 or wider, within the bound.
No kernel may reach another device: no remote copies, remote signals or barrier semaphores. Data moves between devices by JAX's collectives and lax.ppermute only.
A program may use at most 128 MiB of HBM per device.

v0:
```python
import jax
import jax.numpy as jnp
from jax import lax
from jax.sharding import PartitionSpec as P

NGRAM = 2
R_GRP = 8192


learn_rate = 0.5


def shards(
    layer_input,
    norm_gain,
    keyvalue_cotangent,
    keyvalue_weight,
    residual_cotangent,
    ngram_ids,
    table,
    accumulator,
):
    groups = lax.axis_size("group")
    columns = lax.axis_size("col")
    tok_rows = layer_input.shape[0]
    width = layer_input.shape[1]
    slice_width = table.shape[1]
    normed_grad = lax.dot_general(
        keyvalue_cotangent,
        lax.all_gather(keyvalue_weight, "col", axis=0, tiled=True),
        (((1,), (1,)), ((), ())),
        preferred_element_type=jnp.float32,
    )
    values = layer_input.astype(jnp.float32)
    inverse = lax.rsqrt(jnp.mean(values * values, axis=-1, keepdims=True) + 1e-05)
    scaled = normed_grad * norm_gain.astype(jnp.float32)
    inner = jnp.mean(scaled * values, axis=-1, keepdims=True)
    total = (
        inverse * scaled
        - values * (inverse * inverse * inverse) * inner
        + residual_cotangent.astype(jnp.float32)
    )
    token_grad = total.astype(jnp.bfloat16)
    entries = tok_rows * NGRAM
    flat_ids = ngram_ids.reshape(-1)
    order = jnp.arange(entries, dtype=jnp.int32)
    same_row = flat_ids[:, None] == flat_ids[None, :]
    leader = jnp.min(jnp.where(same_row, order[None, :], entries), axis=1)
    is_leader = leader == order
    spread = jnp.broadcast_to(token_grad[:, None, :], (tok_rows, NGRAM, width)).reshape(
        entries, width
    )
    merged = (
        jnp.zeros((entries, width), jnp.float32)
        .at[leader]
        .add(spread.astype(jnp.float32))
        .astype(jnp.bfloat16)
    )
    owners = flat_ids // R_GRP
    local_rows = jnp.where(is_leader, flat_ids - owners * R_GRP, R_GRP)
    onehot = (owners[:, None] == jnp.arange(groups, dtype=jnp.int32)[None, :]).astype(jnp.int32)
    running = jnp.cumsum(onehot, axis=0)
    slots = jnp.sum(running * onehot, axis=1) - 1
    position = owners * tok_rows + slots
    send_rows = jnp.zeros((groups * tok_rows, width), jnp.bfloat16).at[position].set(merged)
    send_ids = jnp.full((groups * tok_rows,), R_GRP, jnp.int32).at[position].set(local_rows)
    laid_rows = send_rows.reshape(groups, tok_rows, columns, slice_width).transpose(0, 2, 1, 3)
    laid_ids = jnp.broadcast_to(send_ids.reshape(groups, 1, tok_rows), (groups, columns, tok_rows))
    arrived, arrived_ids = (
        lax.all_to_all(
            laid_rows.reshape(groups * columns, tok_rows, slice_width),
            ("group", "col"),
            split_axis=0,
            concat_axis=0,
            tiled=True,
        ),
        lax.all_to_all(
            laid_ids.reshape(groups * columns, tok_rows),
            ("group", "col"),
            split_axis=0,
            concat_axis=0,
            tiled=True,
        ),
    )
    dense_grad = (
        jnp.zeros((table.shape[0], slice_width), jnp.float32)
        .at[arrived_ids.reshape(-1)]
        .add(arrived.reshape(-1, slice_width).astype(jnp.float32), mode="drop")
    )
    partial_value = jnp.sum(dense_grad * dense_grad, axis=1)
    squares = lax.psum(partial_value, "col") / width
    new_accum = accumulator + squares
    new_table = table - learn_rate * dense_grad * lax.rsqrt(new_accum)[:, None]
    return (new_table, new_accum)


def solution(mesh):
    in_specs = (
        P(("group", "col"), None),
        P(),
        P(("group", "col"), None),
        P("col", None),
        P(("group", "col"), None),
        P(("group", "col"), None),
        P("group", "col"),
        P("group"),
    )
    out_specs = (P("group", "col"), P("group"))
    return jax.shard_map(shards, mesh=mesh, in_specs=in_specs, out_specs=out_specs, check_vma=False)
```

profile of v0, /device:TPU:0, one launch (start us, length us, event | category | flops | bytes accessed | tf_op | source)
XLA Modules:
  0.0 428.4 jit_solution(6872967317549434843)
XLA Ops:
  7.2 0.7 all-gather.2.cloned.1.call-update
  7.9 0.8 copy.29
  9.2 1.2 reduce-window.6
  11.0 1.4 scatter_custom_fusion
  12.4 0.6 broadcast_in_dim.55
  13.0 11.1 %all-to-all-start = ((s32[128,1,128]{2,1,0:T(1,128)}), s32[128,1,128]{2,1,0:T(1,128)S(1)}, u32[]{:S(2)}, u32[]{:S(2)}) async-start(s32[128,1,128]{2,1,0:T(1,128)} %bitcast.5), calls=%async_computation | async-start | bytes 131072 | tf_op jit(solution)/shard_map/all_to_all | solution.py:77
  24.2 0.7 convert_element_type.35
  24.9 61.2 %all-gather.2.cloned.1.call-done = bf16[4096,2048]{1,0:T(8,128)(2,1)} async-done(((bf16[128,2048]{1,0:T(8,128)(2,1)}), bf16[4096,2048]{1,0:T(8,128)(2,1)}) %all-gather.2.cloned.1.call-update) | async-done | bytes 16777232 | tf_op jit(solution)/shard_map/all_gather | solution.py:30
  86.1 11.7 %fusion.2 = (f32[128]{0:T(128)S(1)}, f32[128]{0:T(128)S(1)}, f32[128,4096]{1,0:T(8,128)S(1)}) fusion(bf16[128,4096]{1,0:T(8,128)(2,1)} %param.8, f32[4096]{0:T(1024)S(1)} %convert_element_type.35, bf16[128,2048]{1,0:T(8,128)(2,1)S(1)} %copy-done, bf16[4096,2048]{1,0:T(8,128)(2,1)} %all-gather.2.cloned.1.call-done), kind=kOutput, calls=%fused_computation.13 | convolution fusion | flops 2150629376 | bytes 20464640 | tf_op jit(solution)/shard_map/dot_general | solution.py:28
  97.8 2.2 fusion.14
  100.0 4.4 %broadcast_in_dim.58 = f32[128,2,4096]{2,1,0:T(2,128)} broadcast(f32[128,4096]{1,0:T(8,128)S(1)} %fusion.14), dimensions={0,2} | broadcast | bytes 6291456 | tf_op jit(solution)/shard_map/broadcast_in_dim | solution.py:50
  104.4 6.1 %reshape.239 = f32[256,4096]{1,0:T(8,128)} reshape(f32[128,2,4096]{2,1,0:T(2,128)} %broadcast_in_dim.58) | data formatting | bytes 8388608 | tf_op jit(solution)/shard_map/convert_element_type | solution.py:56
  110.5 9.9 %scatter_custom_fusion.1 = f32[256,4096]{1,0:T(8,128)} fusion(s32[256]{0:T(256)S(1)} %bitcast.48, f32[256,4096]{1,0:T(8,128)} %reshape.239, f32[]{:T(128)} %constant.15.clone.1), kind=kCustom, calls=%fused_computation.21 | custom fusion | flops 1048576 | bytes 4194816 | tf_op jit(solution)/shard_map/scatter-add | solution.py:56
  120.4 7.6 %scatter_custom_fusion.2 = bf16[512,4096]{1,0:T(8,128)(2,1)} fusion(s32[256]{0:T(256)S(1)} %bitcast.47, f32[256,4096]{1,0:T(8,128)} %scatter_custom_fusion.1, bf16[]{:T(256)} %constant.50.clone.1), kind=kCustom, calls=%fused_computation.19 | custom fusion | flops 1048576 | bytes 8388610 | tf_op jit(solution)/shard_map/scatter | solution.py:65
  128.0 3.4 copy.36
  131.5 0.9 bitcast_bitcast_fusion
  132.4 3.6 copy.34
  136.0 8.6 %all-to-all-start.1 = ((bf16[128,128,128]{2,1,0:T(8,128)(2,1)}), bf16[128,128,128]{2,1,0:T(8,128)(2,1)}, u32[]{:S(2)}, u32[]{:S(2)}) async-start(bf16[128,128,128]{2,1,0:T(8,128)(2,1)} %bitcast.38), calls=%async_computation.1 | async-start | bytes 8388608 | tf_op jit(solution)/shard_map/all_to_all | solution.py:70
  144.7 52.3 %all-to-all-done.1 = bf16[128,128,128]{2,1,0:T(8,128)(2,1)} async-done(((bf16[128,128,128]{2,1,0:T(8,128)(2,1)}), bf16[128,128,128]{2,1,0:T(8,128)(2,1)}, u32[]{:S(2)}, u32[]{:S(2)}) %all-to-all-start.1) | async-done | bytes 4194336 | tf_op jit(solution)/shard_map/all_to_all | solution.py:70
  197.1 90.4 %scatter_custom_fusion.3 = f32[8192,128]{1,0:T(8,128)} fusion(s32[16384]{0:T(1024)S(1)} %bitcast.41, bf16[16384,128]{1,0:T(8,128)(2,1)} %bitcast.13, f32[]{:T(128)} %constant.15.clone.1), kind=kCustom, calls=%fused_computation.4 | custom fusion | flops 4194304 | bytes 8388612 | tf_op jit(solution)/shard_map/scatter-add | solution.py:88
  287.4 3.4 multiply_reduce_fusion
  290.8 124.7 %psum.7 = f32[8192]{0:T(1024)S(1)} all-reduce(f32[8192]{0:T(1024)S(1)} %multiply_reduce_fusion), channel_id=1, replica_groups=mesh['group'=4,'col'=32] {'col'}, use_global_device_ids=true, to_apply=%region_11.12 | all-reduce | flops 8192 | bytes 65536 | tf_op jit(solution)/shard_map/psum | solution.py:91
  415.5 0.6 rsqrt_multiply_fusion
  416.2 5.4 %multiply_subtract_fusion = f32[8192,128]{1,0:T(8,128)} fusion(f32[8192,128]{1,0:T(8,128)} %param.14, f32[8192,128]{1,0:T(8,128)} %scatter_custom_fusion.3, f32[8192]{0:T(1024)S(1)} %get-tuple-element.4), kind=kLoop, calls=%fused_computation.8 | loop fusion | flops 2097152 | bytes 12615680 | tf_op jit(solution)/shard_map/sub | solution.py:93
  (27 shorter events, 1.2 us)
Async XLA Ops:
  7.2 79.0 %copy-start = (bf16[128,2048]{1,0:T(8,128)(2,1)S(1)}, bf16[128,2048]{1,0:T(8,128)(2,1)}, u32[]{:S(2)}) copy-start(bf16[128,2048]{1,0:T(8,128)(2,1)} %param.10) | copy-start | bytes 1572868
  7.2 79.0 %all-gather.2.cloned.1.call-start = ((), (), s32[]{:S(2)}) async-start(), calls=%async_computation.2 | async-start | bytes 17301504 | tf_op jit(solution)/shard_map/all_gather | solution.py:30
  13.0 123.0 %all-to-all-start = ((s32[128,1,128]{2,1,0:T(1,128)}), s32[128,1,128]{2,1,0:T(1,128)S(1)}, u32[]{:S(2)}, u32[]{:S(2)}) async-start(s32[128,1,128]{2,1,0:T(1,128)} %bitcast.5), calls=%async_computation | async-start | bytes 131072 | tf_op jit(solution)/shard_map/all_to_all | solution.py:77
  136.0 61.1 %all-to-all-start.1 = ((bf16[128,128,128]{2,1,0:T(8,128)(2,1)}), bf16[128,128,128]{2,1,0:T(8,128)(2,1)}, u32[]{:S(2)}, u32[]{:S(2)}) async-start(bf16[128,128,128]{2,1,0:T(8,128)(2,1)} %bitcast.38), calls=%async_computation.1 | async-start | bytes 8388608 | tf_op jit(solution)/shard_map/all_to_all | solution.py:70
  287.4 128.1 %copy-start.2 = (f32[8192]{0:T(1024)S(1)}, f32[8192]{0:T(1024)}, u32[]{:S(2)}) copy-start(f32[8192]{0:T(1024)} %param.15) | copy-start | bytes 98308
  416.2 5.5 %copy-start.1 = (bf16[128,2048]{1,0:T(8,128)(2,1)S(1)}, bf16[128,2048]{1,0:T(8,128)(2,1)}, u32[]{:S(2)}) copy-start(bf16[128,2048]{1,0:T(8,128)(2,1)} %param.10) | copy-start | bytes 1572868
Sparse Core Ops, SparseCore 0:
  10.3 75.8 all-gather.1
where the time goes:
time: 429 us; the launch traced here: 428 us
  blocking collectives  125 us (29%)
  other arithmetic  122 us (28%)
  waiting for transfers between devices  114 us (27%)
  local copies, waits for them, and re-layouts  21.9 us (5%)
  starting transfers between devices  19.8 us (5%)
  between operations  14.2 us (3%)
  matrix products  11.7 us (3%)
    psum x1, blocking collectives, shards(): squares = lax.psum(partial_value, 'col') / width  125 us
    scatter-add x1, other arithmetic, shards(): dense_grad = jnp.zeros((table.shape[0], slice_width), jnp.float32).at[arr...  90.4 us
    all_gather x1, waiting for transfers between devices, shards(): lax.all_gather(keyvalue_weight, 'col', axis=0, tiled=True)  61.2 us
    all_to_all x1, waiting for transfers between devices, shards(): lax.all_to_all(laid_rows.reshape(groups * columns, tok_rows, slice_width)...  52.3 us
    dot_general x1, matrix products, shards(): lax.dot_general(keyvalue_cotangent, lax.all_gather(keyvalue_weight, 'col'...  11.7 us
    all_to_all x1, starting transfers between devices, shards(): lax.all_to_all(laid_ids.reshape(groups * columns, tok_rows), ('group', 'c...  11.1 us
    scatter-add x1, other arithmetic, shards(): merged = jnp.zeros((entries, width), jnp.float32).at[leader].add(spread.a...  9.91 us
    all_to_all x1, starting transfers between devices, shards(): lax.all_to_all(laid_rows.reshape(groups * columns, tok_rows, slice_width)...  8.62 us
  transfers between devices with their start and end apart: 3, of which 2 were waited for; matrix products, arithmetic and copies ran while one was open for 13% of the time, Pallas kernels for 0%

commit v1 on v0

v1 whole, which is shorter than its diff:
```python
import functools

import jax
import jax.numpy as jnp
from jax import lax
from jax.experimental import pallas as pl
from jax.experimental.pallas import tpu as pltpu
from jax.sharding import PartitionSpec as P

NGRAM = 2
R_GRP = 8192
PAD = 8
VMEM_LIMIT = 56 * 1024 * 1024
learn_rate = 0.5

NT = (((1,), (1,)), ((), ()))
NN = (((1,), (0,)), ((), ()))


def slots_of(ngram_ids, groups):
    tok = ngram_ids.shape[0]
    ids = ngram_ids.reshape(-1)
    n = ids.shape[0]
    order = jnp.arange(n, dtype=jnp.int32)
    same = ids[:, None] == ids[None, :]
    leader = jnp.min(jnp.where(same, order[None, :], n), axis=1)
    lead = leader == order
    owner = ids // R_GRP
    before = lead[None, :] & (owner[:, None] == owner[None, :]) & (order[None, :] < leader[:, None])
    slot = owner * tok + jnp.sum(before.astype(jnp.int32), axis=1)
    places = jnp.arange(groups * tok, dtype=jnp.int32)
    rows = jnp.min(
        jnp.where(places[:, None] == slot[None, :], (ids - owner * R_GRP)[None, :], R_GRP), axis=1
    )
    return slot.reshape(tok, NGRAM).T, rows.reshape(groups, tok)


def grad_kernel(steps, per, groups, width, cot, w, v, r, gain, slot, out, ng, ss, inner, count):
    i = pl.program_id(0)
    tok = cot.shape[0]
    cols = w.shape[0]

    @pl.when(i == 0)
    def _():
        ss[...] = jnp.zeros_like(ss)
        inner[...] = jnp.zeros_like(inner)
        place = lax.broadcasted_iota(jnp.int32, count.shape, 0)
        total = (place == slot[0:1, :]).astype(jnp.float32)
        for j in range(1, NGRAM):
            total += (place == slot[j : j + 1, :]).astype(jnp.float32)
        count[...] = total.astype(count.dtype)

    @pl.when(i < steps)
    def _():
        at = pl.ds(pl.multiple_of(i * cols, cols), cols)
        part = lax.dot_general(cot[...], w[...], NT, preferred_element_type=jnp.float32)
        scaled = part * gain[:, at].astype(jnp.float32)
        ng[i] = scaled
        values = v[:, at].astype(jnp.float32)
        ss[...] += jnp.sum(values * values, axis=1, keepdims=True)
        inner[...] += jnp.sum(scaled * values, axis=1, keepdims=True)

    @pl.when(i >= steps)
    def _():
        inverse = lax.rsqrt(ss[...] / width + 1e-05)
        cubed = inverse * inverse * inverse
        mean = inner[...] / width
        for k in range(per):
            step = (i - steps) * per + k
            at = pl.ds(pl.multiple_of(step * cols, cols), cols)
            values = v[:, at].astype(jnp.float32)
            total = inverse * ng[step] - values * cubed * mean + r[:, at].astype(jnp.float32)
            merged = lax.dot_general(
                count[...], total.astype(jnp.bfloat16), NN, preferred_element_type=jnp.float32
            ).astype(jnp.bfloat16)
            lanes = out.shape[3]
            for g in range(groups):
                for c in range(cols // lanes):
                    out[g, k * (cols // lanes) + c] = merged[
                        g * tok : (g + 1) * tok, c * lanes : (c + 1) * lanes
                    ]


def merged_rows(cot, w, v, r, gain, slot, groups, columns, lanes):
    tok, width = v.shape
    cols, per = 2 * lanes, 2
    steps = width // cols
    last = steps // per
    whole = lambda i: (0, 0)
    return pl.pallas_call(
        functools.partial(grad_kernel, steps, per, groups, width),
        grid=(steps + last,),
        in_specs=[
            pl.BlockSpec(cot.shape, whole),
            pl.BlockSpec((cols, w.shape[1]), lambda i: (jnp.minimum(i, steps - 1), 0)),
            pl.BlockSpec(v.shape, whole),
            pl.BlockSpec(r.shape, whole),
            pl.BlockSpec((1, width), whole),
            pl.BlockSpec(slot.shape, whole),
        ],
        out_specs=pl.BlockSpec(
            (groups, per * cols // lanes, tok, lanes), lambda i: (0, jnp.maximum(i - steps, 0), 0, 0)
        ),
        out_shape=jax.ShapeDtypeStruct((groups, columns, tok, lanes), jnp.bfloat16),
        scratch_shapes=[
            pltpu.VMEM((steps, tok, cols), jnp.float32),
            pltpu.VMEM((tok, 1), jnp.float32),
            pltpu.VMEM((tok, 1), jnp.float32),
            pltpu.VMEM((groups * tok, tok), jnp.bfloat16),
        ],
        compiler_params=pltpu.CompilerParams(
            dimension_semantics=("arbitrary",), vmem_limit_bytes=VMEM_LIMIT
        ),
        name="grad_merge",
    )(cot, w, v, r, gain.reshape(1, width), slot)


def scatter_kernel(per, batch, rows, counts, x, grad, sq, wide):
    i = pl.program_id(0)
    tok = x.shape[1]

    @pl.when(i == 0)
    def _():
        grad[...] = jnp.zeros_like(grad)

    for k in range(per):
        wide[k] = x[k].astype(jnp.float32)

    def block(k, carry):
        b = i * per + k
        n = counts[b]

        def some(j, carry):
            base = j * batch
            at = [rows[b, base + s] for s in range(batch)]
            old = [grad[pl.ds(at[s], 1), :] for s in range(batch)]
            new = [old[s] + wide[k, pl.ds(base + s, 1), :] for s in range(batch)]
            for s in range(batch):
                grad[pl.ds(at[s], 1), :] = new[s]
            return carry

        return lax.fori_loop(0, (n + batch - 1) // batch, some, carry)

    lax.fori_loop(0, per, block, 0)

    @pl.when(i == pl.num_programs(0) - 1)
    def _():
        ones = jnp.ones((8, grad.shape[1]), jnp.float32)

        def sums(j, carry):
            g = grad[pl.ds(pl.multiple_of(j * tok, tok), tok), :]
            s = lax.dot_general(
                ones,
                g * g,
                NT,
                preferred_element_type=jnp.float32,
                precision=lax.Precision.HIGHEST,
            )
            sq[pl.ds(j, 1), :] = s[0:1, :]
            return carry

        lax.fori_loop(0, sq.shape[0], sums, 0)


def scattered(arrived, rows, counts):
    blocks, tok, lanes = arrived.shape
    per = 8
    return pl.pallas_call(
        functools.partial(scatter_kernel, per, 16),
        grid_spec=pltpu.PrefetchScalarGridSpec(
            num_scalar_prefetch=2,
            grid=(blocks // per,),
            in_specs=[pl.BlockSpec((per, tok, lanes), lambda i, *_: (i, 0, 0))],
            out_specs=[
                pl.BlockSpec((R_GRP + PAD, lanes), lambda i, *_: (0, 0)),
                pl.BlockSpec((R_GRP // lanes, lanes), lambda i, *_: (0, 0)),
            ],
            scratch_shapes=[pltpu.VMEM((per, tok, lanes), jnp.float32)],
        ),
        out_shape=[
            jax.ShapeDtypeStruct((R_GRP + PAD, lanes), jnp.float32),
            jax.ShapeDtypeStruct((R_GRP // lanes, lanes), jnp.float32),
        ],
        compiler_params=pltpu.CompilerParams(
            dimension_semantics=("arbitrary",), vmem_limit_bytes=VMEM_LIMIT
        ),
        name="scatter_rows",
    )(rows, counts, arrived)


def update_kernel(table, grad, scale, out):
    lanes = scale.shape[1]
    for j in range(scale.shape[0]):
        at = pl.ds(j * lanes, lanes)
        wide = jnp.transpose(jnp.broadcast_to(scale[j : j + 1, :], (lanes, lanes)))
        out[at, :] = table[at, :] - learn_rate * grad[at, :] * wide


def updated(table, grad, scale):
    rows, lanes = table.shape
    tile = 1024
    return pl.pallas_call(
        update_kernel,
        grid=(rows // tile,),
        in_specs=[
            pl.BlockSpec((tile, lanes), lambda i: (i, 0)),
            pl.BlockSpec((tile, lanes), lambda i: (i, 0)),
            pl.BlockSpec((tile // lanes, lanes), lambda i: (i, 0)),
        ],
        out_specs=pl.BlockSpec((tile, lanes), lambda i: (i, 0)),
        out_shape=jax.ShapeDtypeStruct(table.shape, table.dtype),
        compiler_params=pltpu.CompilerParams(dimension_semantics=("arbitrary",)),
        name="update_rows",
    )(table, grad, scale)


def col_sum(x):
    def shifted(value, inner_size, size, by):
        pairs = []
        for d in range(lax.axis_size("col")):
            low, high = d % inner_size, d // inner_size
            mid, top = high % size, high // size
            pairs.append((d, (top * size + (mid + by) % size) * inner_size + low))
        return lax.ppermute(value, "col", pairs)

    x = x + shifted(x, 1, 2, 1)
    for inner_size in (2, 8):
        first, second, third = (shifted(x, inner_size, 4, by) for by in (1, 3, 2))
        x = (x + third) + (first + second)
    return x


def shards(
    layer_input,
    norm_gain,
    keyvalue_cotangent,
    keyvalue_weight,
    residual_cotangent,
    ngram_ids,
    table,
    accumulator,
):
    groups, columns = lax.axis_size("group"), lax.axis_size("col")
    tok, width = layer_input.shape
    lanes = table.shape[1]
    weight = lax.all_gather(keyvalue_weight, "col", axis=0, tiled=True)
    slot, rows = slots_of(ngram_ids, groups)
    sent_rows = jnp.broadcast_to(rows[:, None, :], (groups, columns, tok))
    got_rows = lax.all_to_all(
        sent_rows.reshape(groups * columns, tok), ("group", "col"), 0, 0, tiled=True
    )
    counts = jnp.sum((got_rows < R_GRP).astype(jnp.int32), axis=1)
    merged = merged_rows(
        keyvalue_cotangent,
        weight,
        layer_input,
        residual_cotangent,
        norm_gain,
        slot,
        groups,
        columns,
        lanes,
    )
    arrived = lax.all_to_all(
        merged.reshape(groups * columns, tok, lanes), ("group", "col"), 0, 0, tiled=True
    )
    grad, partial = scattered(arrived, got_rows, counts)
    squares = col_sum(partial) / width
    new_accum = accumulator.reshape(squares.shape) + squares
    new_table = updated(table, grad, lax.rsqrt(new_accum))
    return (new_table, new_accum.reshape(-1))


def solution(mesh):
    in_specs = (
        P(("group", "col"), None),
        P(),
        P(("group", "col"), None),
        P("col", None),
        P(("group", "col"), None),
        P(("group", "col"), None),
        P("group", "col"),
        P("group"),
    )
    out_specs = (P("group", "col"), P("group"))
    return jax.shard_map(shards, mesh=mesh, in_specs=in_specs, out_specs=out_specs, check_vma=False)
```

time: 429 us -> 276 us (0.64)
  the two profiles are of different devices: /device:TPU:0 before, /device:TPU:22 now
where the time goes in v1:
time: 276 us; the launch traced here: 275 us
  waiting for transfers between devices  125 us (45%)
  Pallas kernels  105 us (38%)
  starting transfers between devices  23.7 us (9%)
  between operations  14.1 us (5%)
  other arithmetic  3.98 us (1%)
  local copies, waits for them, and re-layouts  3.07 us (1%)
    pallas_call x1, Pallas kernels, scattered(): pl.pallas_call(functools.partial(scatter_kernel, per, 16), grid_spec=pltp...  75.2 us
    all_gather x1, waiting for transfers between devices, shards(): weight = lax.all_gather(keyvalue_weight, 'col', axis=0, tiled=True)  61.9 us
    all_to_all x1, waiting for transfers between devices, shards(): lax.all_to_all(merged.reshape(groups * columns, tok, lanes), ('group', 'c...  49.8 us
    pallas_call x1, Pallas kernels, merged_rows(): pl.pallas_call(functools.partial(grad_kernel, steps, per, groups, width),...  21.8 us
    ppermute x7, waiting for transfers between devices, shifted(): return lax.ppermute(value, 'col', pairs)  12.2 us
    all_to_all x1, starting transfers between devices, shards(): lax.all_to_all(sent_rows.reshape(groups * columns, tok), ('group', 'col')...  10.3 us
    pallas_call x1, Pallas kernels, updated(): pl.pallas_call(update_kernel, grid=(rows // tile,), in_specs=[pl.BlockSpe...  8.04 us
    all_to_all x1, starting transfers between devices, shards(): lax.all_to_all(merged.reshape(groups * columns, tok, lanes), ('group', 'c...  8.01 us
  transfers between devices with their start and end apart: 10, of which 8 were waited for; matrix products, arithmetic and copies ran while one was open for 2% of the time, Pallas kernels for 8%

profile of v1, /device:TPU:22, one launch (start us, length us, event | category | flops | bytes accessed | tf_op | source)
XLA Modules:
  0.0 274.5 jit_solution(7848078332449077980)
XLA Ops:
  7.2 0.7 all-gather.2.cloned.1.call-update
  7.9 0.8 copy.14
  9.4 0.6 broadcast_in_dim.48
  10.1 10.3 %all-to-all-start = ((s32[128,1,128]{2,1,0:T(1,128)}), s32[128,1,128]{2,1,0:T(1,128)S(1)}, u32[]{:S(2)}, u32[]{:S(2)}) async-start(s32[128,1,128]{2,1,0:T(1,128)} %bitcast.1), calls=%async_computation | async-start | bytes 131072 | tf_op jit(solution)/shard_map/all_to_all | solution.py:249
  20.5 1.3 add_bitcast_fusion.slot
  21.8 1.3 reshape.119.gain
  23.2 61.9 %all-gather.2.cloned.1.call-done.w = bf16[4096,2048]{1,0:T(8,128)(2,1)} async-done(((bf16[128,2048]{1,0:T(8,128)(2,1)}), bf16[4096,2048]{1,0:T(8,128)(2,1)}) %all-gather.2.cloned.1.call-update) | async-done | bytes 16777232 | tf_op jit(solution)/shard_map/all_gather | solution.py:246
  85.0 21.8 %grad_merge.1 = bf16[4,32,128,128]{3,2,1,0:T(8,128)(2,1)} custom-call(bf16[128,2048]{1,0:T(8,128)(2,1)} %cot.1, bf16[4096,2048]{1,0:T(8,128)(2,1)} %all-gather.2.cloned.1.call-done.w, bf16[128,4096]{1,0:T(8,128)(2,1)} %v.1, bf16[128,4096]{1,0:T(8,128)(2,1)} %r.1, bf16[1,4096]{1,0:T(2,128)(2,1)} %reshape.119.gain, s32[2,128]{1,0:T(2,128)} %add_bitcast_fusion.slot), custom_call_target="tpu_custom_call" | custom-call | tf_op jit(solution)/shard_map/grad_merge/pallas_call | solution.py:90
  106.9 8.0 %all-to-all-start.1 = ((bf16[128,128,128]{2,1,0:T(8,128)(2,1)}), bf16[128,128,128]{2,1,0:T(8,128)(2,1)}, u32[]{:S(2)}, u32[]{:S(2)}) async-start(bf16[128,128,128]{2,1,0:T(8,128)(2,1)} %bitcast.10), calls=%async_computation.1 | async-start | bytes 8388608 | tf_op jit(solution)/shard_map/all_to_all | solution.py:264
  114.9 0.7 convert_reduce_fusion.1.counts
  115.6 49.8 %all-to-all-done.1.x = bf16[128,128,128]{2,1,0:T(8,128)(2,1)} async-done(((bf16[128,128,128]{2,1,0:T(8,128)(2,1)}), bf16[128,128,128]{2,1,0:T(8,128)(2,1)}, u32[]{:S(2)}, u32[]{:S(2)}) %all-to-all-start.1) | async-done | bytes 4194336 | tf_op jit(solution)/shard_map/all_to_all | solution.py:264
  165.4 75.2 %scatter_rows.1 = (f32[8200,128]{1,0:T(8,128)}, f32[64,128]{1,0:T(8,128)}) custom-call(s32[128,128]{1,0:T(8,128)} %bitcast.12, s32[128]{0:T(128)} %convert_reduce_fusion.1.counts, bf16[128,128,128]{2,1,0:T(8,128)(2,1)} %all-to-all-done.1.x), custom_call_target="tpu_custom_call" | custom-call | tf_op jit(solution)/shard_map/scatter_rows/pallas_call | solution.py:168
  240.6 1.4 collective-permute-done
  242.0 0.8 add.52
  242.8 3.2 %collective-permute-start.2 = (f32[64,128]{1,0:T(8,128)S(1)}, f32[64,128]{1,0:T(8,128)S(1)}, u32[]{:S(2)}, u32[]{:S(2)}) collective-permute-start(f32[64,128]{1,0:T(8,128)S(1)} %add.52), channel_id=1, source_target_pairs={{0,2},{1,3},{2,4},{3,5},{4,6},{5,7},{6,0},{7,1},{8,10},{9,11},{10,... | collective-permute-start | bytes 98312 | tf_op jit(solution)/shard_map/ppermute | solution.py:224
  246.1 1.9 collective-permute-done.3
  247.9 3.5 %collective-permute-done.1 = f32[64,128]{1,0:T(8,128)S(1)} collective-permute-done((f32[64,128]{1,0:T(8,128)S(1)}, f32[64,128]{1,0:T(8,128)S(1)}, u32[]{:S(2)}, u32[]{:S(2)}) %collective-permute-start.1) | collective-permute-done | bytes 32800 | tf_op jit(solution)/shard_map/ppermute | solution.py:224
  251.5 0.5 collective-permute-start.6
  252.0 1.6 collective-permute-start.5
  253.6 1.9 collective-permute-done.6
  255.5 1.7 collective-permute-done.5
  257.1 1.9 collective-permute-done.4
  259.0 0.6 fusion.1
  259.6 8.0 %update_rows.1 = f32[8192,128]{1,0:T(8,128)} custom-call(f32[8192,128]{1,0:T(8,128)} %table.1, f32[8200,128]{1,0:T(8,128)} %get-tuple-element.4.grad, f32[64,128]{1,0:T(8,128)} %get-tuple-element.6.scale), custom_call_target="tpu_custom_call" | custom-call | tf_op jit(solution)/shard_map/update_rows/pallas_call | solution.py:202
  (21 shorter events, 1.0 us)
Async XLA Ops:
  7.2 77.9 %all-gather.2.cloned.1.call-start = ((), (), s32[]{:S(2)}) async-start(), calls=%async_computation.2 | async-start | bytes 17301504 | tf_op jit(solution)/shard_map/all_gather | solution.py:246
  10.1 96.8 %all-to-all-start = ((s32[128,1,128]{2,1,0:T(1,128)}), s32[128,1,128]{2,1,0:T(1,128)S(1)}, u32[]{:S(2)}, u32[]{:S(2)}) async-start(s32[128,1,128]{2,1,0:T(1,128)} %bitcast.1), calls=%async_computation | async-start | bytes 131072 | tf_op jit(solution)/shard_map/all_to_all | solution.py:249
  106.9 8.0 %copy-start = (s32[128,1,128]{2,1,0:T(1,128)}, s32[128,1,128]{2,1,0:T(1,128)S(1)}, u32[]{:S(2)}) copy-start(s32[128,1,128]{2,1,0:T(1,128)S(1)} %all-to-all-done) | copy-start | bytes 196612
  106.9 58.5 %all-to-all-start.1 = ((bf16[128,128,128]{2,1,0:T(8,128)(2,1)}), bf16[128,128,128]{2,1,0:T(8,128)(2,1)}, u32[]{:S(2)}, u32[]{:S(2)}) async-start(bf16[128,128,128]{2,1,0:T(8,128)(2,1)} %bitcast.10), calls=%async_computation.1 | async-start | bytes 8388608 | tf_op jit(solution)/shard_map/all_to_all | solution.py:264
  114.9 144.1 %copy-start.1 = (f32[8192]{0:T(1024)S(1)}, f32[8192]{0:T(1024)}, u32[]{:S(2)}) copy-start(f32[8192]{0:T(1024)} %param.15) | copy-start | bytes 98308
  240.6 1.4 collective-permute-start
  242.8 5.1 %collective-permute-start.3 = (f32[64,128]{1,0:T(8,128)S(1)}, f32[64,128]{1,0:T(8,128)S(1)}, u32[]{:S(2)}, u32[]{:S(2)}) collective-permute-start(f32[64,128]{1,0:T(8,128)S(1)} %add.52), channel_id=1, source_target_pairs={{0,6},{1,7},{2,0},{3,1},{4,2},{5,3},{6,4},{7,5},{8,14},{9,15},{10,... | collective-permute-start | bytes 98312 | tf_op jit(solution)/shard_map/ppermute | solution.py:224
  242.8 5.1 %collective-permute-start.2 = (f32[64,128]{1,0:T(8,128)S(1)}, f32[64,128]{1,0:T(8,128)S(1)}, u32[]{:S(2)}, u32[]{:S(2)}) collective-permute-start(f32[64,128]{1,0:T(8,128)S(1)} %add.52), channel_id=1, source_target_pairs={{0,2},{1,3},{2,4},{3,5},{4,6},{5,7},{6,0},{7,1},{8,10},{9,11},{10,... | collective-permute-start | bytes 98312 | tf_op jit(solution)/shard_map/ppermute | solution.py:224
  246.1 5.4 %collective-permute-start.1 = (f32[64,128]{1,0:T(8,128)S(1)}, f32[64,128]{1,0:T(8,128)S(1)}, u32[]{:S(2)}, u32[]{:S(2)}) collective-permute-start(f32[64,128]{1,0:T(8,128)S(1)} %add.52), channel_id=1, source_target_pairs={{0,4},{1,5},{2,6},{3,7},{4,0},{5,1},{6,2},{7,3},{8,12},{9,13},{10,... | collective-permute-start | bytes 98312 | tf_op jit(solution)/shard_map/ppermute | solution.py:224
  251.5 4.0 %collective-permute-start.6 = (f32[64,128]{1,0:T(8,128)S(1)}, f32[64,128]{1,0:T(8,128)S(1)}, u32[]{:S(2)}, u32[]{:S(2)}) collective-permute-start(f32[64,128]{1,0:T(8,128)S(1)} %add_add_fusion), channel_id=1, source_target_pairs={{0,24},{1,25},{2,26},{3,27},{4,28},{5,29},{6,30},{7,31},{8,0},{9,1... | collective-permute-start | bytes 98312 | tf_op jit(solution)/shard_map/ppermute | solution.py:224
  252.0 5.1 %collective-permute-start.5 = (f32[64,128]{1,0:T(8,128)S(1)}, f32[64,128]{1,0:T(8,128)S(1)}, u32[]{:S(2)}, u32[]{:S(2)}) collective-permute-start(f32[64,128]{1,0:T(8,128)S(1)} %add_add_fusion), channel_id=1, source_target_pairs={{0,8},{1,9},{2,10},{3,11},{4,12},{5,13},{6,14},{7,15},{8,16},{9,17... | collective-permute-start | bytes 98312 | tf_op jit(solution)/shard_map/ppermute | solution.py:224
  253.6 5.4 %collective-permute-start.4 = (f32[64,128]{1,0:T(8,128)S(1)}, f32[64,128]{1,0:T(8,128)S(1)}, u32[]{:S(2)}, u32[]{:S(2)}) collective-permute-start(f32[64,128]{1,0:T(8,128)S(1)} %add_add_fusion), channel_id=1, source_target_pairs={{0,16},{1,17},{2,18},{3,19},{4,20},{5,21},{6,22},{7,23},{8,24},{9,... | collective-permute-start | bytes 98312 | tf_op jit(solution)/shard_map/ppermute | solution.py:224
Sparse Core Ops, SparseCore 0:
  10.3 74.7 all-gather.1

commit v2 on v1

--- a/solution.py
+++ b/solution.py
@@ -128,18 +128,22 @@
 
     def block(k, carry):
         b = i * per + k
-        n = counts[b]
-
-        def some(j, carry):
-            base = j * batch
-            at = [rows[b, base + s] for s in range(batch)]
-            old = [grad[pl.ds(at[s], 1), :] for s in range(batch)]
-            new = [old[s] + wide[k, pl.ds(base + s, 1), :] for s in range(batch)]
-            for s in range(batch):
-                grad[pl.ds(at[s], 1), :] = new[s]
-            return carry
-
-        return lax.fori_loop(0, (n + batch - 1) // batch, some, carry)
+
+        def part(low, high):
+            for first in range(low, high, batch):
+                at = [rows[b * tok + first + s] for s in range(batch)]
+                old = [grad[pl.ds(at[s], 1), :] for s in range(batch)]
+                new = [old[s] + wide[k, pl.ds(first + s, 1), :] for s in range(batch)]
+                for s in range(batch):
+                    grad[pl.ds(at[s], 1), :] = new[s]
+
+        part(0, tok // 2)
+
+        @pl.when(counts[b] > tok // 2)
+        def _():
+            part(tok // 2, tok)
+
+        return carry
 
     lax.fori_loop(0, per, block, 0)
 
@@ -185,7 +189,7 @@
             dimension_semantics=("arbitrary",), vmem_limit_bytes=VMEM_LIMIT
         ),
         name="scatter_rows",
-    )(rows, counts, arrived)
+    )(rows.reshape(-1), counts, arrived)
 
 
 def update_kernel(table, grad, scale, out):

time: 276 us -> 243 us (0.88)
  the two profiles are of different devices: /device:TPU:22 before, /device:TPU:14 now
where the time goes in v2:
time: 243 us; the launch traced here: 242 us
  waiting for transfers between devices  122 us (50%)
  Pallas kernels  72.5 us (30%)
  starting transfers between devices  24.3 us (10%)
  between operations  14.1 us (6%)
  other arithmetic  6.22 us (3%)
  local copies, waits for them, and re-layouts  3.07 us (1%)
    all_gather x1, waiting for transfers between devices, shards(): weight = lax.all_gather(keyvalue_weight, 'col', axis=0, tiled=True)  61.9 us
    all_to_all x1, waiting for transfers between devices, shards(): lax.all_to_all(merged.reshape(groups * columns, tok, lanes), ('group', 'c...  48 us
    pallas_call x1, Pallas kernels, scattered(): pl.pallas_call(functools.partial(scatter_kernel, per, 16), grid_spec=pltp...  42.6 us
    pallas_call x1, Pallas kernels, merged_rows(): pl.pallas_call(functools.partial(grad_kernel, steps, per, groups, width),...  21.8 us
    ppermute x7, waiting for transfers between devices, shifted(): return lax.ppermute(value, 'col', pairs)  11.7 us
    all_to_all x1, starting transfers between devices, shards(): lax.all_to_all(sent_rows.reshape(groups * columns, tok), ('group', 'col')...  10.4 us
    pallas_call x1, Pallas kernels, updated(): pl.pallas_call(update_kernel, grid=(rows // tile,), in_specs=[pl.BlockSpe...  8.04 us
    all_to_all x1, starting transfers between devices, shards(): lax.all_to_all(merged.reshape(groups * columns, tok, lanes), ('group', 'c...  8.01 us
  transfers between devices with their start and end apart: 10, of which 8 were waited for; matrix products, arithmetic and copies ran while one was open for 3% of the time, Pallas kernels for 9%

profile of v2, /device:TPU:14, one launch (start us, length us, event | category | flops | bytes accessed | tf_op | source)
XLA Modules:
  0.0 242.5 jit_solution(7256139203697283820)
XLA Ops:
  7.2 0.7 all-gather.2.cloned.1.call-update
  7.9 0.8 copy.14
  9.4 0.6 broadcast_in_dim.48
  10.1 10.4 %all-to-all-start = ((s32[128,1,128]{2,1,0:T(1,128)}), s32[128,1,128]{2,1,0:T(1,128)S(1)}, u32[]{:S(2)}, u32[]{:S(2)}) async-start(s32[128,1,128]{2,1,0:T(1,128)} %bitcast.1), calls=%async_computation | async-start | bytes 131072 | tf_op jit(solution)/shard_map/all_to_all | solution.py:253
  20.6 1.3 add_bitcast_fusion.slot
  21.9 1.3 reshape.127.gain
  23.2 61.9 %all-gather.2.cloned.1.call-done.w = bf16[4096,2048]{1,0:T(8,128)(2,1)} async-done(((bf16[128,2048]{1,0:T(8,128)(2,1)}), bf16[4096,2048]{1,0:T(8,128)(2,1)}) %all-gather.2.cloned.1.call-update) | async-done | bytes 16777232 | tf_op jit(solution)/shard_map/all_gather | solution.py:250
  85.1 21.8 %grad_merge.1 = bf16[4,32,128,128]{3,2,1,0:T(8,128)(2,1)} custom-call(bf16[128,2048]{1,0:T(8,128)(2,1)} %cot.1, bf16[4096,2048]{1,0:T(8,128)(2,1)} %all-gather.2.cloned.1.call-done.w, bf16[128,4096]{1,0:T(8,128)(2,1)} %v.1, bf16[128,4096]{1,0:T(8,128)(2,1)} %r.1, bf16[1,4096]{1,0:T(2,128)(2,1)} %reshape.127.gain, s32[2,128]{1,0:T(2,128)} %add_bitcast_fusion.slot), custom_call_target="tpu_custom_call" | custom-call | tf_op jit(solution)/shard_map/grad_merge/pallas_call | solution.py:90
  107.0 8.0 %all-to-all-start.1 = ((bf16[128,128,128]{2,1,0:T(8,128)(2,1)}), bf16[128,128,128]{2,1,0:T(8,128)(2,1)}, u32[]{:S(2)}, u32[]{:S(2)}) async-start(bf16[128,128,128]{2,1,0:T(8,128)(2,1)} %bitcast.10), calls=%async_computation.1 | async-start | bytes 8388608 | tf_op jit(solution)/shard_map/all_to_all | solution.py:268
  115.0 2.9 %fusion.1.counts = s32[128]{0:T(128)} fusion(s32[128,1,128]{2,1,0:T(1,128)S(1)} %all-to-all-done), kind=kLoop, calls=%fused_computation.7 | loop fusion | flops 49024 | bytes 66048 | tf_op jit(solution)/shard_map/reduce_sum | solution.py:256
  118.0 48.0 %all-to-all-done.1.x = bf16[128,128,128]{2,1,0:T(8,128)(2,1)} async-done(((bf16[128,128,128]{2,1,0:T(8,128)(2,1)}), bf16[128,128,128]{2,1,0:T(8,128)(2,1)}, u32[]{:S(2)}, u32[]{:S(2)}) %all-to-all-start.1) | async-done | bytes 4194336 | tf_op jit(solution)/shard_map/all_to_all | solution.py:268
  165.9 42.6 %scatter_rows.1 = (f32[8200,128]{1,0:T(8,128)}, f32[64,128]{1,0:T(8,128)}) custom-call(s32[16384]{0:T(1024)} %bitcast.11, s32[128]{0:T(128)} %fusion.1.counts, bf16[128,128,128]{2,1,0:T(8,128)(2,1)} %all-to-all-done.1.x), custom_call_target="tpu_custom_call" | custom-call | tf_op jit(solution)/shard_map/scatter_rows/pallas_call | solution.py:172
  208.6 1.4 collective-permute-done
  210.0 0.8 add.52
  211.2 2.8 %collective-permute-start.2 = (f32[64,128]{1,0:T(8,128)S(1)}, f32[64,128]{1,0:T(8,128)S(1)}, u32[]{:S(2)}, u32[]{:S(2)}) collective-permute-start(f32[64,128]{1,0:T(8,128)S(1)} %add.52), channel_id=1, source_target_pairs={{0,2},{1,3},{2,4},{3,5},{4,6},{5,7},{6,0},{7,1},{8,10},{9,11},{10,... | collective-permute-start | bytes 98312 | tf_op jit(solution)/shard_map/ppermute | solution.py:228
  214.4 1.5 collective-permute-done.3
  215.9 3.5 %collective-permute-done.1 = f32[64,128]{1,0:T(8,128)S(1)} collective-permute-done((f32[64,128]{1,0:T(8,128)S(1)}, f32[64,128]{1,0:T(8,128)S(1)}, u32[]{:S(2)}, u32[]{:S(2)}) %collective-permute-start.1) | collective-permute-done | bytes 32800 | tf_op jit(solution)/shard_map/ppermute | solution.py:228
  219.4 0.8 collective-permute-start.6
  220.2 1.3 collective-permute-start.5
  221.7 1.7 collective-permute-done.6
  223.4 1.9 collective-permute-done.5
  225.3 1.6 collective-permute-done.4
  227.0 0.6 fusion.2
  227.6 8.0 %update_rows.1 = f32[8192,128]{1,0:T(8,128)} custom-call(f32[8192,128]{1,0:T(8,128)} %table.1, f32[8200,128]{1,0:T(8,128)} %get-tuple-element.4.grad, f32[64,128]{1,0:T(8,128)} %get-tuple-element.6.scale), custom_call_target="tpu_custom_call" | custom-call | tf_op jit(solution)/shard_map/update_rows/pallas_call | solution.py:206
  (21 shorter events, 2.0 us)
Async XLA Ops:
  7.2 78.0 %all-gather.2.cloned.1.call-start = ((), (), s32[]{:S(2)}) async-start(), calls=%async_computation.2 | async-start | bytes 17301504 | tf_op jit(solution)/shard_map/all_gather | solution.py:250
  10.1 96.9 %all-to-all-start = ((s32[128,1,128]{2,1,0:T(1,128)}), s32[128,1,128]{2,1,0:T(1,128)S(1)}, u32[]{:S(2)}, u32[]{:S(2)}) async-start(s32[128,1,128]{2,1,0:T(1,128)} %bitcast.1), calls=%async_computation | async-start | bytes 131072 | tf_op jit(solution)/shard_map/all_to_all | solution.py:253
  107.0 8.0 %copy-start = (s32[128,1,128]{2,1,0:T(1,128)}, s32[128,1,128]{2,1,0:T(1,128)S(1)}, u32[]{:S(2)}) copy-start(s32[128,1,128]{2,1,0:T(1,128)S(1)} %all-to-all-done) | copy-start | bytes 196612
  107.0 59.0 %all-to-all-start.1 = ((bf16[128,128,128]{2,1,0:T(8,128)(2,1)}), bf16[128,128,128]{2,1,0:T(8,128)(2,1)}, u32[]{:S(2)}, u32[]{:S(2)}) async-start(bf16[128,128,128]{2,1,0:T(8,128)(2,1)} %bitcast.10), calls=%async_computation.1 | async-start | bytes 8388608 | tf_op jit(solution)/shard_map/all_to_all | solution.py:268
  115.0 111.9 %copy-start.1 = (f32[8192]{0:T(1024)S(1)}, f32[8192]{0:T(1024)}, u32[]{:S(2)}) copy-start(f32[8192]{0:T(1024)} %param.15) | copy-start | bytes 98308
  208.6 1.4 collective-permute-start
  210.8 5.1 %collective-permute-start.3 = (f32[64,128]{1,0:T(8,128)S(1)}, f32[64,128]{1,0:T(8,128)S(1)}, u32[]{:S(2)}, u32[]{:S(2)}) collective-permute-start(f32[64,128]{1,0:T(8,128)S(1)} %add.52), channel_id=1, source_target_pairs={{0,6},{1,7},{2,0},{3,1},{4,2},{5,3},{6,4},{7,5},{8,14},{9,15},{10,... | collective-permute-start | bytes 98312 | tf_op jit(solution)/shard_map/ppermute | solution.py:228
  211.2 4.7 %collective-permute-start.2 = (f32[64,128]{1,0:T(8,128)S(1)}, f32[64,128]{1,0:T(8,128)S(1)}, u32[]{:S(2)}, u32[]{:S(2)}) collective-permute-start(f32[64,128]{1,0:T(8,128)S(1)} %add.52), channel_id=1, source_target_pairs={{0,2},{1,3},{2,4},{3,5},{4,6},{5,7},{6,0},{7,1},{8,10},{9,11},{10,... | collective-permute-start | bytes 98312 | tf_op jit(solution)/shard_map/ppermute | solution.py:228
  214.0 5.4 %collective-permute-start.1 = (f32[64,128]{1,0:T(8,128)S(1)}, f32[64,128]{1,0:T(8,128)S(1)}, u32[]{:S(2)}, u32[]{:S(2)}) collective-permute-start(f32[64,128]{1,0:T(8,128)S(1)} %add.52), channel_id=1, source_target_pairs={{0,4},{1,5},{2,6},{3,7},{4,0},{5,1},{6,2},{7,3},{8,12},{9,13},{10,... | collective-permute-start | bytes 98312 | tf_op jit(solution)/shard_map/ppermute | solution.py:228
  219.4 4.0 %collective-permute-start.6 = (f32[64,128]{1,0:T(8,128)S(1)}, f32[64,128]{1,0:T(8,128)S(1)}, u32[]{:S(2)}, u32[]{:S(2)}) collective-permute-start(f32[64,128]{1,0:T(8,128)S(1)} %add_add_fusion), channel_id=1, source_target_pairs={{0,24},{1,25},{2,26},{3,27},{4,28},{5,29},{6,30},{7,31},{8,0},{9,1... | collective-permute-start | bytes 98312 | tf_op jit(solution)/shard_map/ppermute | solution.py:228
  220.2 5.1 %collective-permute-start.5 = (f32[64,128]{1,0:T(8,128)S(1)}, f32[64,128]{1,0:T(8,128)S(1)}, u32[]{:S(2)}, u32[]{:S(2)}) collective-permute-start(f32[64,128]{1,0:T(8,128)S(1)} %add_add_fusion), channel_id=1, source_target_pairs={{0,8},{1,9},{2,10},{3,11},{4,12},{5,13},{6,14},{7,15},{8,16},{9,17... | collective-permute-start | bytes 98312 | tf_op jit(solution)/shard_map/ppermute | solution.py:228
  221.5 5.4 %collective-permute-start.4 = (f32[64,128]{1,0:T(8,128)S(1)}, f32[64,128]{1,0:T(8,128)S(1)}, u32[]{:S(2)}, u32[]{:S(2)}) collective-permute-start(f32[64,128]{1,0:T(8,128)S(1)} %add_add_fusion), channel_id=1, source_target_pairs={{0,16},{1,17},{2,18},{3,19},{4,20},{5,21},{6,22},{7,23},{8,24},{9,... | collective-permute-start | bytes 98312 | tf_op jit(solution)/shard_map/ppermute | solution.py:228
Sparse Core Ops, SparseCore 0:
  10.3 74.8 all-gather.1

commit v3 on v2

v3 whole, which is shorter than its diff:
```python
import functools

import jax
import jax.numpy as jnp
from jax import lax
from jax.experimental import pallas as pl
from jax.experimental.pallas import tpu as pltpu
from jax.sharding import PartitionSpec as P

NGRAM = 2
R_GRP = 8192
PAD = 8
VMEM_LIMIT = 56 * 1024 * 1024
learn_rate = 0.5

NT = (((1,), (1,)), ((), ()))
NN = (((1,), (0,)), ((), ()))


def slots_of(ngram_ids, groups):
    tok = ngram_ids.shape[0]
    ids = ngram_ids.reshape(-1)
    n = ids.shape[0]
    order = jnp.arange(n, dtype=jnp.int32)
    same = ids[:, None] == ids[None, :]
    leader = jnp.min(jnp.where(same, order[None, :], n), axis=1)
    lead = leader == order
    owner = ids // R_GRP
    before = lead[None, :] & (owner[:, None] == owner[None, :]) & (order[None, :] < leader[:, None])
    slot = jnp.sum(before.astype(jnp.int32), axis=1)
    places = jnp.arange(groups * tok, dtype=jnp.int32)
    rows = jnp.min(
        jnp.where(
            places[:, None] == (owner * tok + slot)[None, :], (ids - owner * R_GRP)[None, :], R_GRP
        ),
        axis=1,
    )
    mine = owner[None, :] == jnp.arange(groups, dtype=jnp.int32)[:, None]
    maps = jnp.where(mine, slot[None, :], -1).reshape(groups, tok, NGRAM)
    parts = [rows.reshape(groups, tok)] + [maps[:, :, j] for j in range(NGRAM)]
    return jnp.concatenate(parts, axis=1)


def grad_kernel(steps, per, width, cot, w, v, r, gain, out, ng, ss, inner):
    i = pl.program_id(0)
    cols = w.shape[0]

    @pl.when(i == 0)
    def _():
        ss[...] = jnp.zeros_like(ss)
        inner[...] = jnp.zeros_like(inner)

    @pl.when(i < steps)
    def _():
        at = pl.ds(pl.multiple_of(i * cols, cols), cols)
        part = lax.dot_general(cot[...], w[...], NT, preferred_element_type=jnp.float32)
        scaled = part * gain[:, at].astype(jnp.float32)
        ng[i] = scaled
        values = v[:, at].astype(jnp.float32)
        ss[...] += jnp.sum(values * values, axis=1, keepdims=True)
        inner[...] += jnp.sum(scaled * values, axis=1, keepdims=True)

    @pl.when(i >= steps)
    def _():
        inverse = lax.rsqrt(ss[...] / width + 1e-05)
        cubed = inverse * inverse * inverse
        mean = inner[...] / width
        for k in range(per):
            step = (i - steps) * per + k
            at = pl.ds(pl.multiple_of(step * cols, cols), cols)
            values = v[:, at].astype(jnp.float32)
            total = inverse * ng[step] - values * cubed * mean + r[:, at].astype(jnp.float32)
            total = total.astype(jnp.bfloat16)
            lanes = out.shape[2]
            for c in range(cols // lanes):
                out[k * (cols // lanes) + c] = total[:, c * lanes : (c + 1) * lanes]


def token_grads(cot, w, v, r, gain, columns, lanes):
    tok, width = v.shape
    cols, per = 2 * lanes, 2
    steps = width // cols
    last = steps // per
    whole = lambda i: (0, 0)
    return pl.pallas_call(
        functools.partial(grad_kernel, steps, per, width),
        grid=(steps + last,),
        in_specs=[
            pl.BlockSpec(cot.shape, whole),
            pl.BlockSpec((cols, w.shape[1]), lambda i: (jnp.minimum(i, steps - 1), 0)),
            pl.BlockSpec(v.shape, whole),
            pl.BlockSpec(r.shape, whole),
            pl.BlockSpec((1, width), whole),
        ],
        out_specs=pl.BlockSpec(
            (per * cols // lanes, tok, lanes), lambda i: (jnp.maximum(i - steps, 0), 0, 0)
        ),
        out_shape=jax.ShapeDtypeStruct((columns, tok, lanes), jnp.bfloat16),
        scratch_shapes=[
            pltpu.VMEM((steps, tok, cols), jnp.float32),
            pltpu.VMEM((tok, 1), jnp.float32),
            pltpu.VMEM((tok, 1), jnp.float32),
        ],
        compiler_params=pltpu.CompilerParams(
            dimension_semantics=("arbitrary",), vmem_limit_bytes=VMEM_LIMIT
        ),
        name="token_grads",
    )(cot, w, v, r, gain.reshape(1, width))


def scatter_kernel(first, last, parts, per, batch, rows, counts, *refs):
    i = pl.program_id(0)
    n = len(parts)
    xs, maps = refs[:n], refs[n]
    if first:
        grad = refs[n + 1]
    else:
        held, grad = refs[n + 1], refs[n + 2]
    wide = refs[-1]
    tok, lanes = wide.shape[1], wide.shape[2]

    @pl.when(i == 0)
    def _():
        grad[...] = jnp.zeros_like(grad) if first else held[...]

    place = lax.broadcasted_iota(jnp.int32, (tok, tok), 0)

    def merge(x):
        for k in range(per):
            total = (place == maps[k, 0:1, :]).astype(jnp.float32)
            for j in range(1, NGRAM):
                total += (place == maps[k, j : j + 1, :]).astype(jnp.float32)
            wide[k] = (
                lax.dot_general(
                    total.astype(jnp.bfloat16), x[k], NN, preferred_element_type=jnp.float32
                )
                .astype(jnp.bfloat16)
                .astype(jnp.float32)
            )

    start = 0
    for p in range(n):
        pl.when((i >= start) & (i < start + parts[p]))(functools.partial(merge, xs[p]))
        start += parts[p]

    def block(k, carry):
        b = i * per + k

        def part(low, high):
            for base in range(low, high, batch):
                at = [rows[b * tok + base + s] for s in range(batch)]
                old = [grad[pl.ds(at[s], 1), :] for s in range(batch)]
                new = [old[s] + wide[k, pl.ds(base + s, 1), :] for s in range(batch)]
                for s in range(batch):
                    grad[pl.ds(at[s], 1), :] = new[s]

        part(0, tok // 2)

        @pl.when(counts[b] > tok // 2)
        def _():
            part(tok // 2, tok)

        return carry

    lax.fori_loop(0, per, block, 0)

    if last:
        sq = refs[n + 3]

        @pl.when(i == pl.num_programs(0) - 1)
        def _():
            ones = jnp.ones((8, lanes), jnp.float32)

            def sums(j, carry):
                g = grad[pl.ds(pl.multiple_of(j * tok, tok), tok), :]
                s = lax.dot_general(
                    ones,
                    g * g,
                    NT,
                    preferred_element_type=jnp.float32,
                    precision=lax.Precision.HIGHEST,
                )
                sq[pl.ds(j, 1), :] = s[0:1, :]
                return carry

            lax.fori_loop(0, sq.shape[0], sums, 0)


def scattered(xs, maps, rows, counts, held, last):
    tok, lanes = xs[0].shape[1:]
    per = 8
    parts = [x.shape[0] // per for x in xs]
    starts = [sum(parts[:p]) for p in range(len(parts))]

    def piece(p):
        return lambda i, *_: (jnp.clip(i - starts[p], 0, parts[p] - 1), 0, 0)

    total = (R_GRP + PAD, lanes)
    in_specs = [pl.BlockSpec((per, tok, lanes), piece(p)) for p in range(len(xs))]
    in_specs.append(pl.BlockSpec((per, NGRAM, tok), lambda i, *_: (i, 0, 0)))
    args = [rows.reshape(-1), counts, *xs, maps]
    whole = lambda i, *_: (0, 0)
    if held is not None:
        in_specs.append(pl.BlockSpec(total, whole))
        args.append(held)
    out_specs = [pl.BlockSpec(total, whole)]
    out_shape = [jax.ShapeDtypeStruct(total, jnp.float32)]
    if last:
        out_specs.append(pl.BlockSpec((R_GRP // lanes, lanes), whole))
        out_shape.append(jax.ShapeDtypeStruct((R_GRP // lanes, lanes), jnp.float32))
    return pl.pallas_call(
        functools.partial(scatter_kernel, held is None, last, parts, per, 16),
        grid_spec=pltpu.PrefetchScalarGridSpec(
            num_scalar_prefetch=2,
            grid=(sum(parts),),
            in_specs=in_specs,
            out_specs=out_specs,
            scratch_shapes=[pltpu.VMEM((per, tok, lanes), jnp.float32)],
        ),
        out_shape=out_shape,
        input_output_aliases={} if held is None else {len(args) - 1: 0},
        compiler_params=pltpu.CompilerParams(
            dimension_semantics=("arbitrary",), vmem_limit_bytes=28 * 1024 * 1024
        ),
        cost_estimate=pl.CostEstimate(
            flops=1000000, bytes_accessed=900000 * sum(x.shape[0] for x in xs), transcendentals=0
        ),
        name="scatter_rows",
    )(*args)


def ring(x, by):
    n = lax.axis_size("group")
    return lax.ppermute(x, "group", [(d, (d + by) % n) for d in range(n)])


def update_kernel(table, grad, scale, out):
    lanes = scale.shape[1]
    for j in range(scale.shape[0]):
        at = pl.ds(j * lanes, lanes)
        wide = jnp.transpose(jnp.broadcast_to(scale[j : j + 1, :], (lanes, lanes)))
        out[at, :] = table[at, :] - learn_rate * grad[at, :] * wide


def updated(table, grad, scale):
    rows, lanes = table.shape
    tile = 1024
    return pl.pallas_call(
        update_kernel,
        grid=(rows // tile,),
        in_specs=[
            pl.BlockSpec((tile, lanes), lambda i: (i, 0)),
            pl.BlockSpec((tile, lanes), lambda i: (i, 0)),
            pl.BlockSpec((tile // lanes, lanes), lambda i: (i, 0)),
        ],
        out_specs=pl.BlockSpec((tile, lanes), lambda i: (i, 0)),
        out_shape=jax.ShapeDtypeStruct(table.shape, table.dtype),
        compiler_params=pltpu.CompilerParams(dimension_semantics=("arbitrary",)),
        name="update_rows",
    )(table, grad, scale)


def col_sum(x):
    def shifted(value, inner_size, size, by):
        pairs = []
        for d in range(lax.axis_size("col")):
            low, high = d % inner_size, d // inner_size
            mid, top = high % size, high // size
            pairs.append((d, (top * size + (mid + by) % size) * inner_size + low))
        return lax.ppermute(value, "col", pairs)

    x = x + shifted(x, 1, 2, 1)
    for inner_size in (2, 8):
        first, second, third = (shifted(x, inner_size, 4, by) for by in (1, 3, 2))
        x = (x + third) + (first + second)
    return x


def shards(
    layer_input,
    norm_gain,
    keyvalue_cotangent,
    keyvalue_weight,
    residual_cotangent,
    ngram_ids,
    table,
    accumulator,
):
    groups, columns = lax.axis_size("group"), lax.axis_size("col")
    tok, width = layer_input.shape
    lanes = table.shape[1]
    weight = lax.all_gather(keyvalue_weight, "col", axis=0, tiled=True)
    plan = slots_of(ngram_ids, groups)
    sent = jnp.broadcast_to(plan[:, None, :], (groups, columns, plan.shape[1]))
    got = lax.all_to_all(
        sent.reshape(groups * columns, -1), ("group", "col"), 0, 0, tiled=True
    ).reshape(groups, columns, -1)
    me = lax.axis_index("group")
    got = [lax.dynamic_index_in_dim(got, (me + by) % groups, 0, False) for by in (0, 3, 1, 2)]
    got = [got[0], jnp.concatenate(got[1:3]), got[3]]
    rows = [g[:, :tok] for g in got]
    maps = [g[:, tok:].reshape(-1, NGRAM, tok) for g in got]
    counts = [jnp.sum((r < R_GRP).astype(jnp.int32), axis=1) for r in rows]
    cotangent, rows, maps, counts = lax.optimization_barrier(
        (keyvalue_cotangent, rows, maps, counts)
    )
    grads = token_grads(
        cotangent,
        weight,
        layer_input,
        residual_cotangent,
        norm_gain,
        columns,
        lanes,
    )
    own = lax.all_to_all(grads, "col", 0, 0, tiled=True)
    half = columns // 2
    left, right = ring(own, 1), ring(own, 3)
    (grad,) = scattered((own,), maps[0], rows[0], counts[0], None, False)
    left, right, grad = lax.optimization_barrier((left, right, grad))
    far = (ring(left[:half], 1), ring(right[half:], 3))
    (grad,) = scattered(
        (left, right),
        maps[1],
        rows[1],
        counts[1],
        grad,
        False,
    )
    grad, partial = scattered(far, maps[2], rows[2], counts[2], grad, True)
    squares = col_sum(partial) / width
    new_accum = accumulator.reshape(squares.shape) + squares
    new_table = updated(table, grad, lax.rsqrt(new_accum))
    return (new_table, new_accum.reshape(-1))


def solution(mesh):
    in_specs = (
        P(("group", "col"), None),
        P(),
        P(("group", "col"), None),
        P("col", None),
        P(("group", "col"), None),
        P(("group", "col"), None),
        P("group", "col"),
        P("group"),
    )
    out_specs = (P("group", "col"), P("group"))
    return jax.shard_map(shards, mesh=mesh, in_specs=in_specs, out_specs=out_specs, check_vma=False)
```

time: 243 us -> 229 us (0.942)
  waiting for transfers between devices: 122 us -> 90.5 us
  blocking collectives: 0 us -> 20.3 us
  other arithmetic: 6.22 us -> 2.18 us
  local copies, waits for them, and re-layouts: 3.07 us -> 5.51 us
    all_to_all x2 -> x1, waiting for transfers between devices: 48 us -> 7.85 us  [shards(): lax.all_to_all(sent.reshape(groups * columns, -1), ('group', 'col'), 0, 0...]
    all_to_all x0 -> x1, blocking collectives: none -> 20.3 us  [shards(): own = lax.all_to_all(grads, 'col', 0, 0, tiled=True)]
    ppermute x0 -> x4, waiting for transfers between devices: none -> 17.1 us  [ring(): return lax.ppermute(x, 'group', [(d, (d + by) % n) for d in range(n)])]
    all_to_all x2 -> x1, starting transfers between devices: 18.4 us -> 10.4 us  [shards(): lax.all_to_all(sent.reshape(groups * columns, -1), ('group', 'col'), 0, 0...]
    all_gather x1, waiting for transfers between devices: 61.9 us -> 54.6 us  [shards(): weight = lax.all_gather(keyvalue_weight, 'col', axis=0, tiled=True)]
    ppermute x0 -> x4, starting transfers between devices: none -> 5.61 us  [ring(): return lax.ppermute(x, 'group', [(d, (d + by) % n) for d in range(n)])]
    reduce_sum x2 -> x3, other arithmetic: 3.16 us -> 0.44 us  [the longest x2 0.23 us: shards(): counts = [jnp.sum((r < R_GRP).astype(jnp.int32), axis=1) for r in rows]]
    pallas_call x2 -> x4, Pallas kernels: 64.5 us -> 64.8 us  [the longest x3 44.9 us: scattered(): pl.pallas_call(functools.partial(scatter_kernel, held is None, last, part...]
  transfers between devices with their start and end apart: 10 -> 13, of which waited for: 8 -> 10; matrix products, arithmetic and copies ran while one was open for 3% -> 2% of each run, Pallas kernels for 9% -> 10%
where the time goes in v3:
time: 229 us
  waiting for transfers between devices  90.5 us (40%)
  Pallas kernels  72.9 us (32%)
  starting transfers between devices  23.1 us (10%)
  blocking collectives  20.3 us (9%)
  between operations  14.3 us (6%)
  local copies, waits for them, and re-layouts  5.51 us (2%)
    all_gather x1, waiting for transfers between devices, shards(): weight = lax.all_gather(keyvalue_weight, 'col', axis=0, tiled=True)  54.6 us
    pallas_call x3, Pallas kernels, scattered(): pl.pallas_call(functools.partial(scatter_kernel, held is None, last, part...  44.9 us
    all_to_all x1, blocking collectives, shards(): own = lax.all_to_all(grads, 'col', 0, 0, tiled=True)  20.3 us
    pallas_call x1, Pallas kernels, token_grads(): pl.pallas_call(functools.partial(grad_kernel, steps, per, width), grid=(s...  19.9 us
    ppermute x4, waiting for transfers between devices, ring(): return lax.ppermute(x, 'group', [(d, (d + by) % n) for d in range(n)])  17.1 us
    all_to_all x1, starting transfers between devices, shards(): lax.all_to_all(sent.reshape(groups * columns, -1), ('group', 'col'), 0, 0...  10.4 us
    ppermute x7, waiting for transfers between devices, shifted(): return lax.ppermute(value, 'col', pairs)  10.3 us
    pallas_call x1, Pallas kernels, updated(): pl.pallas_call(update_kernel, grid=(rows // tile,), in_specs=[pl.BlockSpe...  8.04 us
  transfers between devices with their start and end apart: 13, of which 10 were waited for; matrix products, arithmetic and copies ran while one was open for 2% of the time, Pallas kernels for 10%

profile of v3, /device:TPU:14, one launch (start us, length us, event | category | flops | bytes accessed | tf_op | source)
XLA Modules:
  0.0 228.8 jit_solution(13365989506714676419)
XLA Ops:
  11.3 10.4 %all-to-all-start = ((s32[128,1,384]{2,1,0:T(1,128)}), s32[128,1,384]{2,1,0:T(1,128)S(1)}, u32[]{:S(2)}, u32[]{:S(2)}) async-start(s32[128,1,384]{2,1,0:T(1,128)} %all_to_all.9), calls=%async_computation | async-start | bytes 393216 | tf_op jit(solution)/shard_map/all_to_all | solution.py:295
  21.7 1.3 reshape.160.gain
  23.0 7.8 %all-to-all-done = s32[128,1,384]{2,1,0:T(1,128)S(1)} async-done(((s32[128,1,384]{2,1,0:T(1,128)}), s32[128,1,384]{2,1,0:T(1,128)S(1)}, u32[]{:S(2)}, u32[]{:S(2)}) %all-to-all-start) | async-done | bytes 196640 | tf_op jit(solution)/shard_map/all_to_all | solution.py:295
  31.3 54.6 %all-gather.2.cloned.1.call-done.w = bf16[4096,2048]{1,0:T(8,128)(2,1)} async-done(((bf16[128,2048]{1,0:T(8,128)(2,1)}), bf16[4096,2048]{1,0:T(8,128)(2,1)}) %all-gather.2.cloned.1.call-update) | async-done | bytes 16777232 | tf_op jit(solution)/shard_map/all_gather | solution.py:292
  85.9 19.9 %token_grads.1 = bf16[32,128,128]{2,1,0:T(8,128)(2,1)} custom-call(bf16[128,2048]{1,0:T(8,128)(2,1)} %cot, bf16[4096,2048]{1,0:T(8,128)(2,1)} %all-gather.2.cloned.1.call-done.w, bf16[128,4096]{1,0:T(8,128)(2,1)} %v.1, bf16[128,4096]{1,0:T(8,128)(2,1)} %r.1, bf16[1,4096]{1,0:T(2,128)(2,1)} %reshape.160.gain), custom_call_target="tpu_custom_call" | custom-call | tf_op jit(solution)/shard_map/token_grads/pallas_call | solution.py:85
  105.7 20.3 %all_to_all.14.refs_0_ = bf16[32,128,128]{2,1,0:T(8,128)(2,1)S(1)} all-to-all(bf16[32,128,128]{2,1,0:T(8,128)(2,1)} %token_grads.1), channel_id=1, replica_groups=mesh['group'=4,'col'=32] {'col'}, dimensions={0} | all-to-all | bytes 2097152 | tf_op jit(solution)/shard_map/all_to_all | solution.py:316
  126.6 1.5 collective-permute-start
  128.1 7.8 %scatter_rows.3.refs_3_ = f32[8200,128]{1,0:T(8,128)S(1)} custom-call(s32[4096]{0:T(1024)S(1)} %bitcast.23, s32[32]{0:T(128)S(1)} %get-tuple-element.21.counts, bf16[32,128,128]{2,1,0:T(8,128)(2,1)S(1)} %all_to_all.14.refs_0_, s32[32,2,128]{2,1,0:T(2,128)S(1)} %reshape.156.refs_1_), custom_call_target="tpu_custom_call" | custom-call | flops 1000000 | bytes 28800000 | tf_op jit(solution)/shard_map/scatter_rows/pallas_call | solution.py:211
  135.9 15.9 %collective-permute-done.1.refs_1_ = bf16[32,128,128]{2,1,0:T(8,128)(2,1)S(1)} collective-permute-done((bf16[32,128,128]{2,1,0:T(8,128)(2,1)S(1)}, bf16[32,128,128]{2,1,0:T(8,128)(2,1)S(1)}, u32[]{:S(2)}, u32[]{:S(2)}) %collective-permute-start.1) | collective-permute-done | bytes 1048608 | tf_op jit(solution)/shard_map/ppermute | solution.py:234
  151.8 1.3 collective-permute-done.refs_0_
  153.1 1.0 collective-permute-start.2
  154.2 2.5 %collective-permute-start.3 = (bf16[16,128,128]{2,1,0:T(8,128)(2,1)S(1)}, bf16[16,128,128]{2,1,0:T(8,128)(2,1)S(1)}, u32[]{:S(2)}, u32[]{:S(2)}) collective-permute-start(bf16[16,128,128]{2,1,0:T(8,128)(2,1)S(1)} %slice.39), channel_id=1, source_target_pairs={{0,96},{32,0},{64,32},{96,64},{1,97},{33,1},{65,33},{97,65},{2,98}... | collective-permute-start | bytes 1572872 | tf_op jit(solution)/shard_map/ppermute | solution.py:234
  156.7 15.1 %scatter_rows.4.refs_3_ = f32[8200,128]{1,0:T(8,128)S(1)} custom-call(s32[8192]{0:T(1024)S(1)} %bitcast.21, s32[64]{0:T(128)S(1)} %get-tuple-element.27.counts, bf16[32,128,128]{2,1,0:T(8,128)(2,1)S(1)} %collective-permute-done.refs_0_, bf16[32,128,128]{2,1,0:T(8,128)(2,1)S(1)} %collective-permute-done.1.refs_1_, ...), custom_call_target="tpu_custom_call", output_to_operand_aliasing={{}: (5, {})} | custom-call | flops 1000000 | bytes 57600000 | tf_op jit(solution)/shard_map/scatter_rows/pallas_call | solution.py:211
  171.8 22.1 %scatter_rows.5 = (f32[8200,128]{1,0:T(8,128)S(1)}, f32[64,128]{1,0:T(8,128)S(1)}) custom-call(s32[4096]{0:T(1024)S(1)} %bitcast.22, s32[32]{0:T(128)S(1)} %get-tuple-element.18.counts, bf16[16,128,128]{2,1,0:T(8,128)(2,1)S(1)} %collective-permute-done.2.refs_0_, ...), custom_call_target="tpu_custom_call", output_to_operand_aliasing={{0}: (5, {})} | custom-call | flops 1000000 | bytes 28800000 | tf_op jit(solution)/shard_map/scatter_rows/pallas_call | solution.py:211
  193.9 2.0 copy-done
  195.9 1.2 collective-permute-done.4
  197.6 2.8 %collective-permute-start.6 = (f32[64,128]{1,0:T(8,128)S(1)}, f32[64,128]{1,0:T(8,128)S(1)}, u32[]{:S(2)}, u32[]{:S(2)}) collective-permute-start(f32[64,128]{1,0:T(8,128)S(1)} %add.94), channel_id=1, source_target_pairs={{0,2},{1,3},{2,4},{3,5},{4,6},{5,7},{6,0},{7,1},{8,10},{9,11},{10,... | collective-permute-start | bytes 98312 | tf_op jit(solution)/shard_map/ppermute | solution.py:270
  201.1 1.1 collective-permute-done.7
  202.2 3.5 %collective-permute-done.5 = f32[64,128]{1,0:T(8,128)S(1)} collective-permute-done((f32[64,128]{1,0:T(8,128)S(1)}, f32[64,128]{1,0:T(8,128)S(1)}, u32[]{:S(2)}, u32[]{:S(2)}) %collective-permute-start.5) | collective-permute-done | bytes 32800 | tf_op jit(solution)/shard_map/ppermute | solution.py:270
  205.7 1.5 collective-permute-start.10
  207.8 1.0 collective-permute-start.8
  208.8 0.9 collective-permute-done.10
  209.7 2.7 %collective-permute-done.9 = f32[64,128]{1,0:T(8,128)S(1)} collective-permute-done((f32[64,128]{1,0:T(8,128)S(1)}, f32[64,128]{1,0:T(8,128)S(1)}, u32[]{:S(2)}, u32[]{:S(2)}) %collective-permute-start.9) | collective-permute-done | bytes 32800 | tf_op jit(solution)/shard_map/ppermute | solution.py:270
  213.9 8.0 %update_rows.1 = f32[8192,128]{1,0:T(8,128)} custom-call(f32[8192,128]{1,0:T(8,128)} %table.1, f32[8200,128]{1,0:T(8,128)} %copy-done, f32[64,128]{1,0:T(8,128)} %get-tuple-element.32.scale), custom_call_target="tpu_custom_call" | custom-call | tf_op jit(solution)/shard_map/update_rows/pallas_call | solution.py:248
  (45 shorter events, 8.4 us)
Async XLA Ops:
  7.2 78.7 %all-gather.2.cloned.1.call-start = ((), (), s32[]{:S(2)}) async-start(), calls=%async_computation.2 | async-start | bytes 17301504 | tf_op jit(solution)/shard_map/all_gather | solution.py:292
  11.3 19.6 %all-to-all-start = ((s32[128,1,384]{2,1,0:T(1,128)}), s32[128,1,384]{2,1,0:T(1,128)S(1)}, u32[]{:S(2)}, u32[]{:S(2)}) async-start(s32[128,1,384]{2,1,0:T(1,128)} %all_to_all.9), calls=%async_computation | async-start | bytes 393216 | tf_op jit(solution)/shard_map/all_to_all | solution.py:295
  126.1 25.7 %collective-permute-start.1 = (bf16[32,128,128]{2,1,0:T(8,128)(2,1)S(1)}, bf16[32,128,128]{2,1,0:T(8,128)(2,1)S(1)}, u32[]{:S(2)}, u32[]{:S(2)}) collective-permute-start(bf16[32,128,128]{2,1,0:T(8,128)(2,1)S(1)} %all_to_all.14.refs_0_), channel_id=1, source_target_pairs={{0,96},{32,0},{64,32},{96,64},{1,97},{33,1},{65,33},{97,65},{2,98}... | collective-permute-start | bytes 3145736 | tf_op jit(solution)/shard_map/ppermute | solution.py:234
  126.6 26.4 %collective-permute-start = (bf16[32,128,128]{2,1,0:T(8,128)(2,1)S(1)}, bf16[32,128,128]{2,1,0:T(8,128)(2,1)S(1)}, u32[]{:S(2)}, u32[]{:S(2)}) collective-permute-start(bf16[32,128,128]{2,1,0:T(8,128)(2,1)S(1)} %all_to_all.14.refs_0_), channel_id=1, source_target_pairs={{0,32},{32,64},{64,96},{96,0},{1,33},{33,65},{65,97},{97,1},{2,34}... | collective-permute-start | bytes 3145736 | tf_op jit(solution)/shard_map/ppermute | solution.py:234
  153.1 18.7 %collective-permute-start.2 = (bf16[16,128,128]{2,1,0:T(8,128)(2,1)S(1)}, bf16[16,128,128]{2,1,0:T(8,128)(2,1)S(1)}, u32[]{:S(2)}, u32[]{:S(2)}) collective-permute-start(bf16[16,128,128]{2,1,0:T(8,128)(2,1)S(1)} %slice.38), channel_id=1, source_target_pairs={{0,32},{32,64},{64,96},{96,0},{1,33},{33,65},{65,97},{97,1},{2,34}... | collective-permute-start | bytes 1572872 | tf_op jit(solution)/shard_map/ppermute | solution.py:234
  154.2 17.6 %collective-permute-start.3 = (bf16[16,128,128]{2,1,0:T(8,128)(2,1)S(1)}, bf16[16,128,128]{2,1,0:T(8,128)(2,1)S(1)}, u32[]{:S(2)}, u32[]{:S(2)}) collective-permute-start(bf16[16,128,128]{2,1,0:T(8,128)(2,1)S(1)} %slice.39), channel_id=1, source_target_pairs={{0,96},{32,0},{64,32},{96,64},{1,97},{33,1},{65,33},{97,65},{2,98}... | collective-permute-start | bytes 1572872 | tf_op jit(solution)/shard_map/ppermute | solution.py:234
  171.8 41.5 %copy-start.1 = (f32[8192]{0:T(1024)S(1)}, f32[8192]{0:T(1024)}, u32[]{:S(2)}) copy-start(f32[8192]{0:T(1024)} %param.15) | copy-start | bytes 98308
  193.9 2.0 copy-start
  195.9 1.2 collective-permute-start.4
  197.1 5.1 %collective-permute-start.7 = (f32[64,128]{1,0:T(8,128)S(1)}, f32[64,128]{1,0:T(8,128)S(1)}, u32[]{:S(2)}, u32[]{:S(2)}) collective-permute-start(f32[64,128]{1,0:T(8,128)S(1)} %add.94), channel_id=1, source_target_pairs={{0,6},{1,7},{2,0},{3,1},{4,2},{5,3},{6,4},{7,5},{8,14},{9,15},{10,... | collective-permute-start | bytes 98312 | tf_op jit(solution)/shard_map/ppermute | solution.py:270
  197.6 4.6 %collective-permute-start.6 = (f32[64,128]{1,0:T(8,128)S(1)}, f32[64,128]{1,0:T(8,128)S(1)}, u32[]{:S(2)}, u32[]{:S(2)}) collective-permute-start(f32[64,128]{1,0:T(8,128)S(1)} %add.94), channel_id=1, source_target_pairs={{0,2},{1,3},{2,4},{3,5},{4,6},{5,7},{6,0},{7,1},{8,10},{9,11},{10,... | collective-permute-start | bytes 98312 | tf_op jit(solution)/shard_map/ppermute | solution.py:270
  200.3 5.4 %collective-permute-start.5 = (f32[64,128]{1,0:T(8,128)S(1)}, f32[64,128]{1,0:T(8,128)S(1)}, u32[]{:S(2)}, u32[]{:S(2)}) collective-permute-start(f32[64,128]{1,0:T(8,128)S(1)} %add.94), channel_id=1, source_target_pairs={{0,4},{1,5},{2,6},{3,7},{4,0},{5,1},{6,2},{7,3},{8,12},{9,13},{10,... | collective-permute-start | bytes 98312 | tf_op jit(solution)/shard_map/ppermute | solution.py:270
  205.7 4.0 %collective-permute-start.10 = (f32[64,128]{1,0:T(8,128)S(1)}, f32[64,128]{1,0:T(8,128)S(1)}, u32[]{:S(2)}, u32[]{:S(2)}) collective-permute-start(f32[64,128]{1,0:T(8,128)S(1)} %add_add_fusion), channel_id=1, source_target_pairs={{0,24},{1,25},{2,26},{3,27},{4,28},{5,29},{6,30},{7,31},{8,0},{9,1... | collective-permute-start | bytes 98312 | tf_op jit(solution)/shard_map/ppermute | solution.py:270
  207.3 5.1 %collective-permute-start.9 = (f32[64,128]{1,0:T(8,128)S(1)}, f32[64,128]{1,0:T(8,128)S(1)}, u32[]{:S(2)}, u32[]{:S(2)}) collective-permute-start(f32[64,128]{1,0:T(8,128)S(1)} %add_add_fusion), channel_id=1, source_target_pairs={{0,8},{1,9},{2,10},{3,11},{4,12},{5,13},{6,14},{7,15},{8,16},{9,17... | collective-permute-start | bytes 98312 | tf_op jit(solution)/shard_map/ppermute | solution.py:270
  207.8 5.4 %collective-permute-start.8 = (f32[64,128]{1,0:T(8,128)S(1)}, f32[64,128]{1,0:T(8,128)S(1)}, u32[]{:S(2)}, u32[]{:S(2)}) collective-permute-start(f32[64,128]{1,0:T(8,128)S(1)} %add_add_fusion), channel_id=1, source_target_pairs={{0,16},{1,17},{2,18},{3,19},{4,20},{5,21},{6,22},{7,23},{8,24},{9,... | collective-permute-start | bytes 98312 | tf_op jit(solution)/shard_map/ppermute | solution.py:270
Sparse Core Ops, SparseCore 0:
  10.3 75.5 all-gather.1

commit v4 on v3

v4 whole, which is shorter than its diff:
```python
import functools

import jax
import jax.numpy as jnp
from jax import lax
from jax.experimental import pallas as pl
from jax.experimental.pallas import tpu as pltpu
from jax.sharding import PartitionSpec as P

NGRAM = 2
R_GRP = 8192
PAD = 8
VMEM_LIMIT = 56 * 1024 * 1024
learn_rate = 0.5

NT = (((1,), (1,)), ((), ()))
NN = (((1,), (0,)), ((), ()))


def slots_of(ngram_ids, groups):
    tok = ngram_ids.shape[0]
    ids = ngram_ids.reshape(-1)
    n = ids.shape[0]
    order = jnp.arange(n, dtype=jnp.int32)
    same = ids[:, None] == ids[None, :]
    leader = jnp.min(jnp.where(same, order[None, :], n), axis=1)
    lead = leader == order
    owner = ids // R_GRP
    before = lead[None, :] & (owner[:, None] == owner[None, :]) & (order[None, :] < leader[:, None])
    slot = jnp.sum(before.astype(jnp.int32), axis=1)
    places = jnp.arange(groups * tok, dtype=jnp.int32)
    rows = jnp.min(
        jnp.where(
            places[:, None] == (owner * tok + slot)[None, :], (ids - owner * R_GRP)[None, :], R_GRP
        ),
        axis=1,
    )
    mine = owner[None, :] == jnp.arange(groups, dtype=jnp.int32)[:, None]
    maps = jnp.where(mine, slot[None, :], -1).reshape(groups, tok, NGRAM)
    parts = [rows.reshape(groups, tok)] + [maps[:, :, j] for j in range(NGRAM)]
    return jnp.concatenate(parts, axis=1)


def product_kernel(pieces, first, last, columns, *refs):
    n = len(pieces)
    where, refs = refs[0], refs[1:]
    cot_own, cot_pair = refs[0], refs[1]
    ws = refs[2 : 2 + n]
    tok, deep = cot_own.shape
    depth = deep // 2
    if first:
        v_own, v_pair, ng, ss = refs[2 + n :]
        ng[...] = jnp.zeros_like(ng)
    else:
        held, gain, v_own, v_pair, ng, inner = refs[2 + n :]
        ng[...] = held[...]
    lanes = ng.shape[3]
    for (half, blocks), w in zip(pieces, ws):
        at = slice(half * depth, (half + 1) * depth)
        for k in range(0, len(blocks), 2):
            rows = w[k * lanes : (k + 2) * lanes, :]
            for part, cot in enumerate((cot_own, cot_pair)):
                p = lax.dot_general(cot[:, at], rows, NT, preferred_element_type=jnp.float32)
                for j in range(2):
                    ng[blocks[k + j], part] += p[:, j * lanes : (j + 1) * lanes]
    if first:
        for part, v in enumerate((v_own, v_pair)):

            def squares(j, total):
                x = v[:, pl.ds(pl.multiple_of(j * lanes, lanes), lanes)].astype(jnp.float32)
                return total + x * x

            ss[part] = lax.fori_loop(0, columns, squares, jnp.zeros((tok, lanes), jnp.float32))
    if last:
        for part, v in enumerate((v_own, v_pair)):

            def products(j, total):
                at = pl.ds(pl.multiple_of(where[j] * lanes, lanes), lanes)
                scaled = ng[j, part] * gain[:, at].astype(jnp.float32)
                ng[j, part] = scaled
                return total + scaled * v[:, at].astype(jnp.float32)

            inner[part] = lax.fori_loop(
                0, ng.shape[0], products, jnp.zeros((tok, lanes), jnp.float32)
            )


def finish_kernel(width, where, ng, ss, inner, other, v_own, v_pair, r_own, r_pair, out):
    tok, lanes = ng.shape[2:]
    core = lax.rem(where[0], 2)
    for part, (v, r) in enumerate(((v_own, r_own), (v_pair, r_pair))):
        square = jnp.sum(ss[part], axis=1, keepdims=True)
        inverse = lax.rsqrt(square / width + 1e-05)
        cubed = inverse * inverse * inverse
        mean = jnp.sum(inner[part] + other[1 - part], axis=1, keepdims=True) / width
        place = core if part == 0 else 1 - core

        def block(j, carry):
            at = pl.ds(pl.multiple_of(where[j] * lanes, lanes), lanes)
            values = v[:, at].astype(jnp.float32)
            total = inverse * ng[j, part] - values * cubed * mean + r[:, at].astype(jnp.float32)
            out[lax.div(where[j], 2), place] = total.astype(out.dtype)
            return carry

        lax.fori_loop(0, ng.shape[0], block, 0)


def vmem_call(kernel, n, out_shape, name, aliases=None):
    space = pl.BlockSpec(memory_space=pltpu.VMEM)
    return pl.pallas_call(
        kernel,
        in_specs=[pl.BlockSpec(memory_space=pltpu.SMEM)] + [space] * (n - 1),
        out_specs=jax.tree.map(lambda _: space, out_shape),
        out_shape=out_shape,
        input_output_aliases=aliases or {},
        compiler_params=pltpu.CompilerParams(vmem_limit_bytes=40 * 1024 * 1024),
        name=name,
    )


def shifted(value, inner_size, size, by):
    pairs = []
    for d in range(lax.axis_size("col")):
        low, high = d % inner_size, d // inner_size
        mid, top = high % size, high // size
        pairs.append((d, (top * size + (mid + by) % size) * inner_size + low))
    return lax.ppermute(value, "col", pairs)


def along(x, axis):
    inner_size = {"x": 2, "z": 8}[axis]
    left, right = shifted(x, inner_size, 4, 1), shifted(x, inner_size, 4, 3)
    return left, right


def far_halves(left, right, axis):
    inner_size = {"x": 2, "z": 8}[axis]
    half = left.shape[0] // 2
    return shifted(left[:half], inner_size, 4, 1), shifted(right[half:], inner_size, 4, 3)


def token_grads(cot, w, v, r, gain, lanes):
    columns = lax.axis_size("col")
    tok, width = v.shape
    depth = w.shape[1] // 2
    me = lax.axis_index("col")
    z, x, core = me // 8, (me // 2) % 4, me % 2
    where = jnp.stack(
        [
            (((z + 4 - dz) % 4) * 4 + (x + 4 - dx) % 4) * 2 + core
            for dz in range(4)
            for dx in range(4)
        ]
    ).astype(jnp.int32)
    cot_pair, v_pair, r_pair = (shifted(t, 1, 2, 1) for t in (cot, v, r))
    rows = []
    for half, axis in enumerate("xz"):
        own = w[:, half * depth : (half + 1) * depth]
        left, right = along(own, axis)
        near, farther = far_halves(left, right, axis)
        rows.append(jnp.concatenate([own, left, near, farther, right]))
    sides = [along(rows[0], "z"), along(rows[1], "x")]
    far = [far_halves(*sides[0], "z"), far_halves(*sides[1], "x")]

    def line(half, k, low=0, high=4):
        return (half, [k * 4 + j if half == 0 else j * 4 + k for j in range(low, high)])

    pieces, ws = [], []
    for half in range(2):
        for k, piece in ((0, rows[half]), (1, sides[half][0]), (3, sides[half][1])):
            pieces.append(line(half, k))
            ws.append(piece)
    product = jax.ShapeDtypeStruct((16, 2, tok, lanes), jnp.float32)
    stat = jax.ShapeDtypeStruct((2, tok, lanes), jnp.float32)
    args = (where, cot, cot_pair, *ws, v, v_pair)
    ng, ss = vmem_call(
        functools.partial(product_kernel, pieces, True, False, columns),
        len(args),
        (product, stat),
        "product_near",
    )(*args)
    pieces, ws = [], []
    for half in range(2):
        for low, piece in ((0, far[half][0]), (2, far[half][1])):
            pieces.append(line(half, 2, low, low + 2))
            ws.append(piece)
    args = (where, cot, cot_pair, *ws, ng, gain.reshape(1, width), v, v_pair)
    scaled, inner = vmem_call(
        functools.partial(product_kernel, pieces, False, True, columns),
        len(args),
        (product, stat),
        "product_far",
        {len(args) - 4: 0},
    )(*args)
    other = shifted(inner, 1, 2, 1)
    args = (where, scaled, ss, inner, other, v, v_pair, r, r_pair)
    return vmem_call(
        functools.partial(finish_kernel, width),
        len(args),
        jax.ShapeDtypeStruct((16, 2, tok, lanes), jnp.bfloat16),
        "token_grads",
    )(*args)


def scatter_kernel(first, parts, per, batch, rows, counts, *refs):
    i = pl.program_id(0)
    n = len(parts)
    xs, maps = refs[:n], refs[n]
    if first:
        grad = refs[n + 1]
    else:
        held, grad = refs[n + 1], refs[n + 2]
    wide = refs[-1]
    tok, lanes = wide.shape[1], wide.shape[2]

    @pl.when(i == 0)
    def _():
        grad[...] = jnp.zeros_like(grad) if first else held[...]

    place = lax.broadcasted_iota(jnp.int32, (tok, tok), 0)

    def merge(x):
        for k in range(per):
            total = (place == maps[k, 0:1, :]).astype(jnp.float32)
            for j in range(1, NGRAM):
                total += (place == maps[k, j : j + 1, :]).astype(jnp.float32)
            wide[k] = (
                lax.dot_general(
                    total.astype(jnp.bfloat16), x[k], NN, preferred_element_type=jnp.float32
                )
                .astype(jnp.bfloat16)
                .astype(jnp.float32)
            )

    start = 0
    for p in range(n):
        pl.when((i >= start) & (i < start + parts[p]))(functools.partial(merge, xs[p]))
        start += parts[p]

    def block(k, carry):
        b = i * per + k

        def part(low, high):
            for base in range(low, high, batch):
                at = [rows[b * tok + base + s] for s in range(batch)]
                old = [grad[pl.ds(at[s], 1), :] for s in range(batch)]
                new = [old[s] + wide[k, pl.ds(base + s, 1), :] for s in range(batch)]
                for s in range(batch):
                    grad[pl.ds(at[s], 1), :] = new[s]

        part(0, tok // 2)

        @pl.when(counts[b] > tok // 2)
        def _():
            part(tok // 2, tok)

        return carry

    lax.fori_loop(0, per, block, 0)


def scattered(xs, maps, rows, counts, held):
    tok, lanes = xs[0].shape[1:]
    per = 8
    parts = [x.shape[0] // per for x in xs]
    starts = [sum(parts[:p]) for p in range(len(parts))]

    def piece(p):
        return lambda i, *_: (jnp.clip(i - starts[p], 0, parts[p] - 1), 0, 0)

    total = (R_GRP + PAD, lanes)
    in_specs = [pl.BlockSpec((per, tok, lanes), piece(p)) for p in range(len(xs))]
    in_specs.append(pl.BlockSpec((per, NGRAM, tok), lambda i, *_: (i, 0, 0)))
    args = [rows.reshape(-1), counts, *xs, maps]
    whole = lambda i, *_: (0, 0)
    if held is not None:
        in_specs.append(pl.BlockSpec(total, whole))
        args.append(held)
    return pl.pallas_call(
        functools.partial(scatter_kernel, held is None, parts, per, 16),
        grid_spec=pltpu.PrefetchScalarGridSpec(
            num_scalar_prefetch=2,
            grid=(sum(parts),),
            in_specs=in_specs,
            out_specs=pl.BlockSpec(total, whole),
            scratch_shapes=[pltpu.VMEM((per, tok, lanes), jnp.float32)],
        ),
        out_shape=jax.ShapeDtypeStruct(total, jnp.float32),
        input_output_aliases={} if held is None else {len(args) - 1: 0},
        compiler_params=pltpu.CompilerParams(
            dimension_semantics=("arbitrary",), vmem_limit_bytes=28 * 1024 * 1024
        ),
        cost_estimate=pl.CostEstimate(
            flops=1000000, bytes_accessed=900000 * sum(x.shape[0] for x in xs), transcendentals=0
        ),
        name="scatter_rows",
    )(*args)


def ring(x, by):
    n = lax.axis_size("group")
    return lax.ppermute(x, "group", [(d, (d + by) % n) for d in range(n)])


def col_sum(x):
    x = x + shifted(x, 1, 2, 1)
    for inner_size in (2, 8):
        first, second, third = (shifted(x, inner_size, 4, by) for by in (1, 3, 2))
        x = (x + third) + (first + second)
    return x


def shards(
    layer_input,
    norm_gain,
    keyvalue_cotangent,
    keyvalue_weight,
    residual_cotangent,
    ngram_ids,
    table,
    accumulator,
):
    groups, columns = lax.axis_size("group"), lax.axis_size("col")
    tok, width = layer_input.shape
    lanes = table.shape[1]
    plan = slots_of(ngram_ids, groups)
    sent = jnp.broadcast_to(plan[:, None, :], (groups, columns, plan.shape[1]))
    got = lax.all_to_all(
        sent.reshape(groups * columns, -1), ("group", "col"), 0, 0, tiled=True
    ).reshape(groups, columns, -1)
    me = lax.axis_index("group")
    got = [lax.dynamic_index_in_dim(got, (me + by) % groups, 0, False) for by in (0, 3, 1, 2)]
    got = [got[0], jnp.concatenate(got[1:3]), got[3]]
    rows = [g[:, :tok] for g in got]
    maps = [g[:, tok:].reshape(-1, NGRAM, tok) for g in got]
    counts = [jnp.sum((r < R_GRP).astype(jnp.int32), axis=1) for r in rows]
    cotangent, rows, maps, counts = lax.optimization_barrier(
        (keyvalue_cotangent, rows, maps, counts)
    )
    grads = token_grads(
        cotangent, keyvalue_weight, layer_input, residual_cotangent, norm_gain, lanes
    )
    planes = [[q * 2 + core for q in range(columns // 2)] for core in range(2)]
    own = lax.all_to_all(
        grads.reshape(columns // 2, 2 * tok, lanes),
        "col",
        0,
        0,
        axis_index_groups=planes,
        tiled=True,
    ).reshape(columns, tok, lanes)
    half = columns // 2
    left, right = ring(own, 1), ring(own, 3)
    grad = scattered((own,), maps[0], rows[0], counts[0], None)
    left, right, grad = lax.optimization_barrier((left, right, grad))
    far = (ring(left[:half], 1), ring(right[half:], 3))
    grad = scattered((left, right), maps[1], rows[1], counts[1], grad)
    grad = scattered(far, maps[2], rows[2], counts[2], grad)[:R_GRP]
    partial = jnp.sum(grad * grad, axis=1).reshape(-1, lanes)
    squares = col_sum(partial) / width
    new_accum = accumulator + squares.reshape(-1)
    new_table = table - learn_rate * grad * lax.rsqrt(new_accum)[:, None]
    return (new_table, new_accum)


def solution(mesh):
    in_specs = (
        P(("group", "col"), None),
        P(),
        P(("group", "col"), None),
        P("col", None),
        P(("group", "col"), None),
        P(("group", "col"), None),
        P("group", "col"),
        P("group"),
    )
    out_specs = (P("group", "col"), P("group"))
    return jax.shard_map(shards, mesh=mesh, in_specs=in_specs, out_specs=out_specs, check_vma=False)
```

time: 229 us -> 195 us (0.85)
  the two profiles are of different devices: /device:TPU:14 before, /device:TPU:22 now
where the time goes in v4:
time: 195 us; the launch traced here: 194 us
  waiting for transfers between devices  49.4 us (25%)
  starting transfers between devices  45.8 us (23%)
  Pallas kernels  44.5 us (23%)
  local copies, waits for them, and re-layouts  24.8 us (13%)
  blocking collectives  20.4 us (10%)
  other arithmetic  7.96 us (4%)
    ppermute x27, waiting for transfers between devices, shifted(): return lax.ppermute(value, 'col', pairs)  34.8 us
    ppermute x27, starting transfers between devices, shifted(): return lax.ppermute(value, 'col', pairs)  31.9 us
    pallas_call x3, Pallas kernels, scattered(): pl.pallas_call(functools.partial(scatter_kernel, held is None, parts, per...  30.9 us
    all_to_all x1, blocking collectives, shards(): lax.all_to_all(grads.reshape(columns // 2, 2 * tok, lanes), 'col', 0, 0,...  20.4 us
    ppermute x4, waiting for transfers between devices, ring(): return lax.ppermute(x, 'group', [(d, (d + by) % n) for d in range(n)])  14.6 us
    unnamed x26, local copies, waits for them, and re-layouts  10 us
    all_to_all x1, starting transfers between devices, shards(): lax.all_to_all(sent.reshape(groups * columns, -1), ('group', 'col'), 0, 0...  9.45 us
    pallas_call x1, Pallas kernels, token_grads(): vmem_call(functools.partial(product_kernel, pieces, True, False, columns)...  7.32 us
  transfers between devices with their start and end apart: 32, of which 15 were waited for; matrix products, arithmetic and copies ran while one was open for 10% of the time, Pallas kernels for 18%

profile of v4, /device:TPU:22, one launch (start us, length us, event | category | flops | bytes accessed | tf_op | source)
XLA Modules:
  0.0 194.0 jit_solution(8974001873483477798)
XLA Ops:
  0.6 2.1 %fusion.2 = (bf16[128,1024]{1,0:T(8,128)(2,1)S(1)}, bf16[512,1024]{1,0:T(8,128)(2,1)}, bf16[512,1024]{1,0:T(8,128)(2,1)}, bf16[128,1024]{1,0:T(8,128)(2,1)}) fusion(bf16[128,2048]{1,0:T(8,128)(2,1)} %param.11), kind=kLoop, calls=%fused_computation.47 | loop fusion | bytes 1572864 | tf_op jit(solution)/shard_map/slice | solution.py:158
  2.7 1.9 collective-permute-start.9
  4.6 2.1 %collective-permute-start.11 = (bf16[128,1024]{1,0:T(8,128)(2,1)S(1)}, bf16[128,1024]{1,0:T(8,128)(2,1)S(1)}, u32[]{:S(2)}, u32[]{:S(2)}) collective-permute-start(bf16[128,1024]{1,0:T(8,128)(2,1)S(1)} %get-tuple-element.42), channel_id=1, source_target_pairs={{0,24},{1,25},{2,26},{3,27},{4,28},{5,29},{6,30},{7,31},{8,0},{9,1... | collective-permute-start | bytes 786440 | tf_op jit(solution)/shard_map/ppermute | solution.py:127
  14.1 9.5 %all-to-all-start = ((s32[128,1,384]{2,1,0:T(1,128)}), s32[128,1,384]{2,1,0:T(1,128)S(1)}, u32[]{:S(2)}, u32[]{:S(2)}) async-start(s32[128,1,384]{2,1,0:T(1,128)} %all_to_all.9), calls=%async_computation | async-start | bytes 393216 | tf_op jit(solution)/shard_map/all_to_all | solution.py:328
  23.6 3.5 %collective-permute-start.12 = (bf16[64,1024]{1,0:T(8,128)(2,1)S(1)}, bf16[64,1024]{1,0:T(8,128)(2,1)S(1)}, u32[]{:S(2)}, u32[]{:S(2)}) collective-permute-start(bf16[64,1024]{1,0:T(8,128)(2,1)S(1)} %slice.95), channel_id=1, source_target_pairs={{0,24},{1,25},{2,26},{3,27},{4,28},{5,29},{6,30},{7,31},{8,0},{9,1... | collective-permute-start | bytes 393224 | tf_op jit(solution)/shard_map/ppermute | solution.py:127
  38.3 2.8 %collective-permute-done.4 = bf16[64,1024]{1,0:T(8,128)(2,1)S(1)} collective-permute-done((bf16[64,1024]{1,0:T(8,128)(2,1)S(1)}, bf16[64,1024]{1,0:T(8,128)(2,1)S(1)}, u32[]{:S(2)}, u32[]{:S(2)}) %collective-permute-start.4) | collective-permute-done | bytes 131104 | tf_op jit(solution)/shard_map/ppermute | solution.py:127
  47.5 9.9 %collective-permute-done.13.refs_7_ = bf16[512,1024]{1,0:T(8,128)(2,1)S(1)} collective-permute-done((bf16[512,1024]{1,0:T(8,128)(2,1)}, bf16[512,1024]{1,0:T(8,128)(2,1)S(1)}, u32[]{:S(2)}, u32[]{:S(2)}) %collective-permute-start.13) | collective-permute-done | bytes 1048608 | tf_op jit(solution)/shard_map/ppermute | solution.py:127
  57.4 6.3 %collective-permute-done.15.refs_8_ = bf16[512,1024]{1,0:T(8,128)(2,1)} collective-permute-done((bf16[512,1024]{1,0:T(8,128)(2,1)}, bf16[512,1024]{1,0:T(8,128)(2,1)}, u32[]{:S(2)}, u32[]{:S(2)}) %collective-permute-start.15) | collective-permute-done | bytes 1048608 | tf_op jit(solution)/shard_map/ppermute | solution.py:127
  66.4 3.9 %collective-permute-done.5.refs_4_ = bf16[512,1024]{1,0:T(8,128)(2,1)} collective-permute-done((bf16[512,1024]{1,0:T(8,128)(2,1)}, bf16[512,1024]{1,0:T(8,128)(2,1)}, u32[]{:S(2)}, u32[]{:S(2)}) %collective-permute-start.5) | collective-permute-done | bytes 1048608 | tf_op jit(solution)/shard_map/ppermute | solution.py:127
  72.2 2.0 %collective-permute-start.16 = (bf16[256,1024]{1,0:T(8,128)(2,1)}, bf16[256,1024]{1,0:T(8,128)(2,1)}, u32[]{:S(2)}, u32[]{:S(2)}) collective-permute-start(bf16[256,1024]{1,0:T(8,128)(2,1)} %slice.97), channel_id=1, source_target_pairs={{0,6},{1,7},{2,0},{3,1},{4,2},{5,3},{6,4},{7,5},{8,14},{9,15},{10,... | collective-permute-start | bytes 1572872 | tf_op jit(solution)/shard_map/ppermute | solution.py:127
  76.9 3.2 %collective-permute-start.8 = (bf16[256,1024]{1,0:T(8,128)(2,1)}, bf16[256,1024]{1,0:T(8,128)(2,1)}, u32[]{:S(2)}, u32[]{:S(2)}) collective-permute-start(bf16[256,1024]{1,0:T(8,128)(2,1)} %slice.93), channel_id=1, source_target_pairs={{0,24},{1,25},{2,26},{3,27},{4,28},{5,29},{6,30},{7,31},{8,0},{9,1... | collective-permute-start | bytes 1572872 | tf_op jit(solution)/shard_map/ppermute | solution.py:127
  84.2 7.3 %product_near.1 = (f32[16,2,128,128]{3,2,1,0:T(8,128)S(1)}, f32[2,128,128]{2,1,0:T(8,128)S(1)}) custom-call(s32[16]{0:T(128)S(1)} %stack.67.refs_0_.where, bf16[128,2048]{1,0:T(8,128)(2,1)S(1)} %copy-done.1, bf16[128,2048]{1,0:T(8,128)(2,1)S(1)} %copy-done.3, bf16[512,1024]{1,0:T(8,128)(2,1)S(1)} %copy-done.4, ...), custom_call_target="tpu_custom_call" | custom-call | tf_op jit(solution)/shard_map/product_near/pallas_call | solution.py:176
  91.6 3.9 %product_far.1 = (f32[16,2,128,128]{3,2,1,0:T(8,128)S(1)}, f32[2,128,128]{2,1,0:T(8,128)S(1)}) custom-call(s32[16]{0:T(128)S(1)} %stack.67.refs_0_.where, bf16[128,2048]{1,0:T(8,128)(2,1)S(1)} %copy-done.1, bf16[128,2048]{1,0:T(8,128)(2,1)S(1)} %copy-done.3, bf16[256,1024]{1,0:T(8,128)(2,1)} %collective-permute-done.6.refs_3_, ...), custom_call_target="tpu_custom_call", output_to_operand_aliasing={{0}: (7, {})} | custom-call | tf_op jit(solution)/shard_map/product_far/pallas_call | solution.py:188
  96.9 2.4 %token_grads.1 = bf16[16,2,128,128]{3,2,1,0:T(8,128)(2,1)S(1)} custom-call(s32[16]{0:T(128)S(1)} %stack.67.refs_0_.where, f32[16,2,128,128]{3,2,1,0:T(8,128)S(1)} %get-tuple-element.23.ng, f32[2,128,128]{2,1,0:T(8,128)S(1)} %get-tuple-element.24.ss, f32[2,128,128]{2,1,0:T(8,128)S(1)} %get-tuple-element.25.inner, ...), custom_call_target="tpu_custom_call" | custom-call | tf_op jit(solution)/shard_map/token_grads/pallas_call | solution.py:197
  99.3 20.4 %all_to_all.14 = bf16[16,256,128]{2,1,0:T(8,128)(2,1)S(1)} all-to-all(bf16[16,256,128]{2,1,0:T(8,128)(2,1)S(1)} %bitcast.45), channel_id=1, replica_groups={{0,2,4,6,8,10,12,14,16,18,20,22,24,26,28,30},{1,3,5,7,9,11,13,15,17,19,..., dimensions={0} | all-to-all | bytes 2097152 | tf_op jit(solution)/shard_map/all_to_all | solution.py:344
  121.8 7.8 %scatter_rows.3.refs_3_ = f32[8200,128]{1,0:T(8,128)S(1)} custom-call(s32[4096]{0:T(1024)S(1)} %bitcast.48, s32[32]{0:T(128)S(1)} %get-tuple-element.27.counts, bf16[32,128,128]{2,1,0:T(8,128)(2,1)S(1)} %bitcast.44, s32[32,2,128]{2,1,0:T(2,128)S(1)} %reshape.163.refs_1_), custom_call_target="tpu_custom_call" | custom-call | flops 1000000 | bytes 28800000 | tf_op jit(solution)/shard_map/scatter_rows/pallas_call | solution.py:279
  129.6 13.6 %collective-permute-done.20.refs_0_ = bf16[32,128,128]{2,1,0:T(8,128)(2,1)S(1)} collective-permute-done((bf16[32,128,128]{2,1,0:T(8,128)(2,1)S(1)}, bf16[32,128,128]{2,1,0:T(8,128)(2,1)S(1)}, u32[]{:S(2)}, u32[]{:S(2)}) %collective-permute-start.20) | collective-permute-done | bytes 1048608 | tf_op jit(solution)/shard_map/ppermute | solution.py:302
  144.2 2.4 %collective-permute-start.22 = (bf16[16,128,128]{2,1,0:T(8,128)(2,1)S(1)}, bf16[16,128,128]{2,1,0:T(8,128)(2,1)S(1)}, u32[]{:S(2)}, u32[]{:S(2)}) collective-permute-start(bf16[16,128,128]{2,1,0:T(8,128)(2,1)S(1)} %slice.81), channel_id=1, source_target_pairs={{0,32},{32,64},{64,96},{96,0},{1,33},{33,65},{65,97},{97,1},{2,34}... | collective-permute-start | bytes 1572872 | tf_op jit(solution)/shard_map/ppermute | solution.py:302
  146.7 15.1 %scatter_rows.4.refs_3_ = f32[8200,128]{1,0:T(8,128)S(1)} custom-call(s32[8192]{0:T(1024)S(1)} %bitcast.46, s32[64]{0:T(128)S(1)} %get-tuple-element.33.counts, bf16[32,128,128]{2,1,0:T(8,128)(2,1)S(1)} %collective-permute-done.20.refs_0_, bf16[32,128,128]{2,1,0:T(8,128)(2,1)S(1)} %collective-permute-done.21.refs_1_, ...), custom_call_target="tpu_custom_call", output_to_operand_aliasing={{}: (5, {})} | custom-call | flops 1000000 | bytes 57600000 | tf_op jit(solution)/shard_map/scatter_rows/pallas_call | solution.py:279
  161.8 8.1 %scatter_rows.5 = f32[8200,128]{1,0:T(8,128)S(1)} custom-call(s32[4096]{0:T(1024)S(1)} %bitcast.47, s32[32]{0:T(128)S(1)} %get-tuple-element.20.counts, bf16[16,128,128]{2,1,0:T(8,128)(2,1)S(1)} %collective-permute-done.22.refs_0_, bf16[16,128,128]{2,1,0:T(8,128)(2,1)S(1)} %collective-permute-done.23.refs_1_, ...), custom_call_target="tpu_custom_call", output_to_operand_aliasing={{}: (5, {})} | custom-call | flops 1000000 | bytes 28800000 | tf_op jit(solution)/shard_map/scatter_rows/pallas_call | solution.py:279
  172.3 3.1 %collective-permute-start.25 = (f32[64,128]{1,0:T(8,128)S(1)}, f32[64,128]{1,0:T(8,128)S(1)}, u32[]{:S(2)}, u32[]{:S(2)}) collective-permute-start(f32[64,128]{1,0:T(8,128)S(1)} %bitcast_add_fusion.1), channel_id=1, source_target_pairs={{0,4},{1,5},{2,6},{3,7},{4,0},{5,1},{6,2},{7,3},{8,12},{9,13},{10,... | collective-permute-start | bytes 98312 | tf_op jit(solution)/shard_map/ppermute | solution.py:127
  179.3 2.9 %collective-permute-done.27 = f32[64,128]{1,0:T(8,128)S(1)} collective-permute-done((f32[64,128]{1,0:T(8,128)S(1)}, f32[64,128]{1,0:T(8,128)S(1)}, u32[]{:S(2)}, u32[]{:S(2)}) %collective-permute-start.27) | collective-permute-done | bytes 32800 | tf_op jit(solution)/shard_map/ppermute | solution.py:127
  183.7 3.1 %collective-permute-start.30 = (f32[64,128]{1,0:T(8,128)S(1)}, f32[64,128]{1,0:T(8,128)S(1)}, u32[]{:S(2)}, u32[]{:S(2)}) collective-permute-start(f32[64,128]{1,0:T(8,128)S(1)} %add_add_fusion), channel_id=1, source_target_pairs={{0,24},{1,25},{2,26},{3,27},{4,28},{5,29},{6,30},{7,31},{8,0},{9,1... | collective-permute-start | bytes 98312 | tf_op jit(solution)/shard_map/ppermute | solution.py:127
  189.3 4.7 %multiply_subtract_fusion = f32[8192,128]{1,0:T(8,128)} fusion(f32[8192,128]{1,0:T(8,128)S(1)} %copy-done.6, f32[8200,128]{1,0:T(8,128)S(1)} %scatter_rows.5, f32[8192]{0:T(1024)S(1)} %get-tuple-element.36), kind=kLoop, calls=%fused_computation | loop fusion | flops 2097152 | bytes 12615680 | tf_op jit(solution)/shard_map/sub | solution.py:362
  (117 shorter events, 51.1 us)
Async XLA Ops:
  2.7 10.3 %collective-permute-start.9 = (bf16[128,1024]{1,0:T(8,128)(2,1)S(1)}, bf16[128,1024]{1,0:T(8,128)(2,1)S(1)}, u32[]{:S(2)}, u32[]{:S(2)}) collective-permute-start(bf16[128,1024]{1,0:T(8,128)(2,1)S(1)} %get-tuple-element.42), channel_id=1, source_target_pairs={{0,8},{1,9},{2,10},{3,11},{4,12},{5,13},{6,14},{7,15},{8,16},{9,17... | collective-permute-start | bytes 786440 | tf_op jit(solution)/shard_map/ppermute | solution.py:127
  4.6 18.9 %collective-permute-start.11 = (bf16[128,1024]{1,0:T(8,128)(2,1)S(1)}, bf16[128,1024]{1,0:T(8,128)(2,1)S(1)}, u32[]{:S(2)}, u32[]{:S(2)}) collective-permute-start(bf16[128,1024]{1,0:T(8,128)(2,1)S(1)} %get-tuple-element.42), channel_id=1, source_target_pairs={{0,24},{1,25},{2,26},{3,27},{4,28},{5,29},{6,30},{7,31},{8,0},{9,1... | collective-permute-start | bytes 786440 | tf_op jit(solution)/shard_map/ppermute | solution.py:127
  6.8 20.4 %collective-permute-start.1 = (bf16[128,1024]{1,0:T(8,128)(2,1)}, bf16[128,1024]{1,0:T(8,128)(2,1)S(1)}, u32[]{:S(2)}, u32[]{:S(2)}) collective-permute-start(bf16[128,1024]{1,0:T(8,128)(2,1)} %get-tuple-element.45), channel_id=1, source_target_pairs={{0,2},{1,3},{2,4},{3,5},{4,6},{5,7},{6,0},{7,1},{8,10},{9,11},{10,... | collective-permute-start | bytes 786440 | tf_op jit(solution)/shard_map/ppermute | solution.py:127
  7.2 25.8 %collective-permute-start.3 = (bf16[128,1024]{1,0:T(8,128)(2,1)}, bf16[128,1024]{1,0:T(8,128)(2,1)}, u32[]{:S(2)}, u32[]{:S(2)}) collective-permute-start(bf16[128,1024]{1,0:T(8,128)(2,1)} %get-tuple-element.45), channel_id=1, source_target_pairs={{0,6},{1,7},{2,0},{3,1},{4,2},{5,3},{6,4},{7,5},{8,14},{9,15},{10,... | collective-permute-start | bytes 786440 | tf_op jit(solution)/shard_map/ppermute | solution.py:127
  13.1 16.0 %collective-permute-start.10 = (bf16[64,1024]{1,0:T(8,128)(2,1)S(1)}, bf16[64,1024]{1,0:T(8,128)(2,1)S(1)}, u32[]{:S(2)}, u32[]{:S(2)}) collective-permute-start(bf16[64,1024]{1,0:T(8,128)(2,1)S(1)} %slice.94), channel_id=1, source_target_pairs={{0,8},{1,9},{2,10},{3,11},{4,12},{5,13},{6,14},{7,15},{8,16},{9,17... | collective-permute-start | bytes 393224 | tf_op jit(solution)/shard_map/ppermute | solution.py:127
  14.1 18.9 %all-to-all-start = ((s32[128,1,384]{2,1,0:T(1,128)}), s32[128,1,384]{2,1,0:T(1,128)S(1)}, u32[]{:S(2)}, u32[]{:S(2)}) async-start(s32[128,1,384]{2,1,0:T(1,128)} %all_to_all.9), calls=%async_computation | async-start | bytes 393216 | tf_op jit(solution)/shard_map/all_to_all | solution.py:328
  23.6 7.1 %collective-permute-start.12 = (bf16[64,1024]{1,0:T(8,128)(2,1)S(1)}, bf16[64,1024]{1,0:T(8,128)(2,1)S(1)}, u32[]{:S(2)}, u32[]{:S(2)}) collective-permute-start(bf16[64,1024]{1,0:T(8,128)(2,1)S(1)} %slice.95), channel_id=1, source_target_pairs={{0,24},{1,25},{2,26},{3,27},{4,28},{5,29},{6,30},{7,31},{8,0},{9,1... | collective-permute-start | bytes 393224 | tf_op jit(solution)/shard_map/ppermute | solution.py:127
  27.8 9.9 %collective-permute-start.2 = (bf16[64,1024]{1,0:T(8,128)(2,1)}, bf16[64,1024]{1,0:T(8,128)(2,1)S(1)}, u32[]{:S(2)}, u32[]{:S(2)}) collective-permute-start(bf16[64,1024]{1,0:T(8,128)(2,1)} %slice.90), channel_id=1, source_target_pairs={{0,2},{1,3},{2,4},{3,5},{4,6},{5,7},{6,0},{7,1},{8,10},{9,11},{10,... | collective-permute-start | bytes 393224 | tf_op jit(solution)/shard_map/ppermute | solution.py:127
  32.1 25.3 %collective-permute-start.13 = (bf16[512,1024]{1,0:T(8,128)(2,1)}, bf16[512,1024]{1,0:T(8,128)(2,1)S(1)}, u32[]{:S(2)}, u32[]{:S(2)}) collective-permute-start(bf16[512,1024]{1,0:T(8,128)(2,1)} %constant_dynamic-update-slice_fusion.5.refs_6_), channel_id=1, source_target_pairs={{0,2},{1,3},{2,4},{3,5},{4,6},{5,7},{6,0},{7,1},{8,10},{9,11},{10,... | collective-permute-start | bytes 3145736 | tf_op jit(solution)/shard_map/ppermute | solution.py:127
  33.0 44.0 %collective-permute-start.17 = (bf16[128,4096]{1,0:T(8,128)(2,1)S(1)}, bf16[128,4096]{1,0:T(8,128)(2,1)S(1)}, u32[]{:S(2)}, u32[]{:S(2)}) collective-permute-start(bf16[128,4096]{1,0:T(8,128)(2,1)S(1)} %copy-done), channel_id=1, source_target_pairs={{0,1},{1,0},{2,3},{3,2},{4,5},{5,4},{6,7},{7,6},{8,9},{9,8},{10,11... | collective-permute-start | bytes 3145736 | tf_op jit(solution)/shard_map/ppermute | solution.py:127
  33.9 7.2 %collective-permute-start.4 = (bf16[64,1024]{1,0:T(8,128)(2,1)S(1)}, bf16[64,1024]{1,0:T(8,128)(2,1)S(1)}, u32[]{:S(2)}, u32[]{:S(2)}) collective-permute-start(bf16[64,1024]{1,0:T(8,128)(2,1)S(1)} %slice.91), channel_id=1, source_target_pairs={{0,6},{1,7},{2,0},{3,1},{4,2},{5,3},{6,4},{7,5},{8,14},{9,15},{10,... | collective-permute-start | bytes 393224 | tf_op jit(solution)/shard_map/ppermute | solution.py:127
  36.8 26.9 %collective-permute-start.15 = (bf16[512,1024]{1,0:T(8,128)(2,1)}, bf16[512,1024]{1,0:T(8,128)(2,1)}, u32[]{:S(2)}, u32[]{:S(2)}) collective-permute-start(bf16[512,1024]{1,0:T(8,128)(2,1)} %constant_dynamic-update-slice_fusion.5.refs_6_), channel_id=1, source_target_pairs={{0,6},{1,7},{2,0},{3,1},{4,2},{5,3},{6,4},{7,5},{8,14},{9,15},{10,... | collective-permute-start | bytes 3145736 | tf_op jit(solution)/shard_map/ppermute | solution.py:127
  43.4 26.8 %collective-permute-start.5 = (bf16[512,1024]{1,0:T(8,128)(2,1)}, bf16[512,1024]{1,0:T(8,128)(2,1)}, u32[]{:S(2)}, u32[]{:S(2)}) collective-permute-start(bf16[512,1024]{1,0:T(8,128)(2,1)} %constant_dynamic-update-slice_fusion.refs_3_), channel_id=1, source_target_pairs={{0,8},{1,9},{2,10},{3,11},{4,12},{5,13},{6,14},{7,15},{8,16},{9,17... | collective-permute-start | bytes 3145736 | tf_op jit(solution)/shard_map/ppermute | solution.py:127
  45.2 26.9 %collective-permute-start.7 = (bf16[512,1024]{1,0:T(8,128)(2,1)}, bf16[512,1024]{1,0:T(8,128)(2,1)}, u32[]{:S(2)}, u32[]{:S(2)}) collective-permute-start(bf16[512,1024]{1,0:T(8,128)(2,1)} %constant_dynamic-update-slice_fusion.refs_3_), channel_id=1, source_target_pairs={{0,24},{1,25},{2,26},{3,27},{4,28},{5,29},{6,30},{7,31},{8,0},{9,1... | collective-permute-start | bytes 3145736 | tf_op jit(solution)/shard_map/ppermute | solution.py:127
  57.4 18.6 %collective-permute-start = (bf16[128,2048]{1,0:T(8,128)(2,1)}, bf16[128,2048]{1,0:T(8,128)(2,1)S(1)}, u32[]{:S(2)}, u32[]{:S(2)}) collective-permute-start(bf16[128,2048]{1,0:T(8,128)(2,1)} %refs_1_.1), channel_id=1, source_target_pairs={{0,1},{1,0},{2,3},{3,2},{4,5},{5,4},{6,7},{7,6},{8,9},{9,8},{10,11... | collective-permute-start | bytes 1572872 | tf_op jit(solution)/shard_map/ppermute | solution.py:127
  63.7 31.9 %collective-permute-start.19 = (bf16[128,4096]{1,0:T(8,128)(2,1)}, bf16[128,4096]{1,0:T(8,128)(2,1)}, u32[]{:S(2)}, u32[]{:S(2)}) collective-permute-start(bf16[128,4096]{1,0:T(8,128)(2,1)} %r_own.1), channel_id=1, source_target_pairs={{0,1},{1,0},{2,3},{3,2},{4,5},{5,4},{6,7},{7,6},{8,9},{9,8},{10,11... | collective-permute-start | bytes 3145736 | tf_op jit(solution)/shard_map/ppermute | solution.py:127
  70.3 21.3 %collective-permute-start.14 = (bf16[256,1024]{1,0:T(8,128)(2,1)}, bf16[256,1024]{1,0:T(8,128)(2,1)}, u32[]{:S(2)}, u32[]{:S(2)}) collective-permute-start(bf16[256,1024]{1,0:T(8,128)(2,1)} %slice.96), channel_id=1, source_target_pairs={{0,2},{1,3},{2,4},{3,5},{4,6},{5,7},{6,0},{7,1},{8,10},{9,11},{10,... | collective-permute-start | bytes 1572872 | tf_op jit(solution)/shard_map/ppermute | solution.py:127
  72.2 19.4 %collective-permute-start.16 = (bf16[256,1024]{1,0:T(8,128)(2,1)}, bf16[256,1024]{1,0:T(8,128)(2,1)}, u32[]{:S(2)}, u32[]{:S(2)}) collective-permute-start(bf16[256,1024]{1,0:T(8,128)(2,1)} %slice.97), channel_id=1, source_target_pairs={{0,6},{1,7},{2,0},{3,1},{4,2},{5,3},{6,4},{7,5},{8,14},{9,15},{10,... | collective-permute-start | bytes 1572872 | tf_op jit(solution)/shard_map/ppermute | solution.py:127
  76.8 14.7 %collective-permute-start.6 = (bf16[256,1024]{1,0:T(8,128)(2,1)}, bf16[256,1024]{1,0:T(8,128)(2,1)}, u32[]{:S(2)}, u32[]{:S(2)}) collective-permute-start(bf16[256,1024]{1,0:T(8,128)(2,1)} %slice.92), channel_id=1, source_target_pairs={{0,8},{1,9},{2,10},{3,11},{4,12},{5,13},{6,14},{7,15},{8,16},{9,17... | collective-permute-start | bytes 1572872 | tf_op jit(solution)/shard_map/ppermute | solution.py:127
  76.9 14.7 %collective-permute-start.8 = (bf16[256,1024]{1,0:T(8,128)(2,1)}, bf16[256,1024]{1,0:T(8,128)(2,1)}, u32[]{:S(2)}, u32[]{:S(2)}) collective-permute-start(bf16[256,1024]{1,0:T(8,128)(2,1)} %slice.93), channel_id=1, source_target_pairs={{0,24},{1,25},{2,26},{3,27},{4,28},{5,29},{6,30},{7,31},{8,0},{9,1... | collective-permute-start | bytes 1572872 | tf_op jit(solution)/shard_map/ppermute | solution.py:127
  119.7 23.4 %collective-permute-start.20 = (bf16[32,128,128]{2,1,0:T(8,128)(2,1)S(1)}, bf16[32,128,128]{2,1,0:T(8,128)(2,1)S(1)}, u32[]{:S(2)}, u32[]{:S(2)}) collective-permute-start(bf16[32,128,128]{2,1,0:T(8,128)(2,1)S(1)} %bitcast.42), channel_id=1, source_target_pairs={{0,32},{32,64},{64,96},{96,0},{1,33},{33,65},{65,97},{97,1},{2,34}... | collective-permute-start | bytes 3145736 | tf_op jit(solution)/shard_map/ppermute | solution.py:302
  121.0 23.2 %collective-permute-start.21 = (bf16[32,128,128]{2,1,0:T(8,128)(2,1)S(1)}, bf16[32,128,128]{2,1,0:T(8,128)(2,1)S(1)}, u32[]{:S(2)}, u32[]{:S(2)}) collective-permute-start(bf16[32,128,128]{2,1,0:T(8,128)(2,1)S(1)} %bitcast.43), channel_id=1, source_target_pairs={{0,96},{32,0},{64,32},{96,64},{1,97},{33,1},{65,33},{97,65},{2,98}... | collective-permute-start | bytes 3145736 | tf_op jit(solution)/shard_map/ppermute | solution.py:302
  144.2 17.5 %collective-permute-start.22 = (bf16[16,128,128]{2,1,0:T(8,128)(2,1)S(1)}, bf16[16,128,128]{2,1,0:T(8,128)(2,1)S(1)}, u32[]{:S(2)}, u32[]{:S(2)}) collective-permute-start(bf16[16,128,128]{2,1,0:T(8,128)(2,1)S(1)} %slice.81), channel_id=1, source_target_pairs={{0,32},{32,64},{64,96},{96,0},{1,33},{33,65},{65,97},{97,1},{2,34}... | collective-permute-start | bytes 1572872 | tf_op jit(solution)/shard_map/ppermute | solution.py:302
  146.6 15.2 %collective-permute-start.23 = (bf16[16,128,128]{2,1,0:T(8,128)(2,1)S(1)}, bf16[16,128,128]{2,1,0:T(8,128)(2,1)S(1)}, u32[]{:S(2)}, u32[]{:S(2)}) collective-permute-start(bf16[16,128,128]{2,1,0:T(8,128)(2,1)S(1)} %slice.82), channel_id=1, source_target_pairs={{0,96},{32,0},{64,32},{96,64},{1,97},{33,1},{65,33},{97,65},{2,98}... | collective-permute-start | bytes 1572872 | tf_op jit(solution)/shard_map/ppermute | solution.py:302
  (17 other events, 117.8 us)

commit v5 on v4

--- a/solution.py
+++ b/solution.py
@@ -133,13 +133,7 @@
     return left, right
 
 
-def far_halves(left, right, axis):
-    inner_size = {"x": 2, "z": 8}[axis]
-    half = left.shape[0] // 2
-    return shifted(left[:half], inner_size, 4, 1), shifted(right[half:], inner_size, 4, 3)
-
-
-def token_grads(cot, w, v, r, gain, lanes):
+def token_grads(cot, w, v, r, gain, lanes, plan):
     columns = lax.axis_size("col")
     tok, width = v.shape
     depth = w.shape[1] // 2
@@ -153,25 +147,39 @@
         ]
     ).astype(jnp.int32)
     cot_pair, v_pair, r_pair = (shifted(t, 1, 2, 1) for t in (cot, v, r))
-    rows = []
+    step = {"x": 2, "z": 8}
+    firsts = []
     for half, axis in enumerate("xz"):
         own = w[:, half * depth : (half + 1) * depth]
-        left, right = along(own, axis)
-        near, farther = far_halves(left, right, axis)
-        rows.append(jnp.concatenate([own, left, near, farther, right]))
-    sides = [along(rows[0], "z"), along(rows[1], "x")]
-    far = [far_halves(*sides[0], "z"), far_halves(*sides[1], "x")]
+        firsts.append((own, *along(own, axis)))
+    lows = [jnp.concatenate([own, left]) for own, left, _ in firsts]
+    low_sides = [along(lows[0], "z"), along(lows[1], "x")]
+    highs = []
+    for half, axis in enumerate("xz"):
+        _, left, right = firsts[half]
+        part = left.shape[0] // 2
+        near = shifted(left[:part], step[axis], 4, 1)
+        farther = shifted(right[part:], step[axis], 4, 3)
+        highs.append(jnp.concatenate([near, farther, right]))
+    high_sides = [along(highs[0], "z"), along(highs[1], "x")]
+    far = [
+        (shifted(low_sides[half][0], step[axis], 4, 1), shifted(high_sides[half][1], step[axis], 4, 3))
+        for half, axis in enumerate("zx")
+    ]
 
     def line(half, k, low=0, high=4):
         return (half, [k * 4 + j if half == 0 else j * 4 + k for j in range(low, high)])
 
     pieces, ws = [], []
     for half in range(2):
-        for k, piece in ((0, rows[half]), (1, sides[half][0]), (3, sides[half][1])):
-            pieces.append(line(half, k))
-            ws.append(piece)
+        low_set = (lows[half], *low_sides[half])
+        high_set = (highs[half], *high_sides[half])
+        for k, low, high in zip((0, 1, 3), low_set, high_set):
+            pieces += [line(half, k, 0, 2), line(half, k, 2, 4)]
+            ws += [low, high]
     product = jax.ShapeDtypeStruct((16, 2, tok, lanes), jnp.float32)
     stat = jax.ShapeDtypeStruct((2, tok, lanes), jnp.float32)
+    plan, cot = lax.optimization_barrier((plan, cot))
     args = (where, cot, cot_pair, *ws, v, v_pair)
     ng, ss = vmem_call(
         functools.partial(product_kernel, pieces, True, False, columns),
@@ -194,12 +202,13 @@
     )(*args)
     other = shifted(inner, 1, 2, 1)
     args = (where, scaled, ss, inner, other, v, v_pair, r, r_pair)
-    return vmem_call(
+    grads = vmem_call(
         functools.partial(finish_kernel, width),
         len(args),
         jax.ShapeDtypeStruct((16, 2, tok, lanes), jnp.bfloat16),
         "token_grads",
     )(*args)
+    return grads, plan
 
 
 def scatter_kernel(first, parts, per, batch, rows, counts, *refs):
@@ -323,22 +332,28 @@
     groups, columns = lax.axis_size("group"), lax.axis_size("col")
     tok, width = layer_input.shape
     lanes = table.shape[1]
-    plan = slots_of(ngram_ids, groups)
-    sent = jnp.broadcast_to(plan[:, None, :], (groups, columns, plan.shape[1]))
-    got = lax.all_to_all(
-        sent.reshape(groups * columns, -1), ("group", "col"), 0, 0, tiled=True
-    ).reshape(groups, columns, -1)
-    me = lax.axis_index("group")
-    got = [lax.dynamic_index_in_dim(got, (me + by) % groups, 0, False) for by in (0, 3, 1, 2)]
-    got = [got[0], jnp.concatenate(got[1:3]), got[3]]
-    rows = [g[:, :tok] for g in got]
-    maps = [g[:, tok:].reshape(-1, NGRAM, tok) for g in got]
-    counts = [jnp.sum((r < R_GRP).astype(jnp.int32), axis=1) for r in rows]
-    cotangent, rows, maps, counts = lax.optimization_barrier(
-        (keyvalue_cotangent, rows, maps, counts)
-    )
-    grads = token_grads(
-        cotangent, keyvalue_weight, layer_input, residual_cotangent, norm_gain, lanes
+    def exchange(plan):
+        sent = jnp.broadcast_to(plan[:, None, :], (groups, columns, plan.shape[1]))
+        got = lax.all_to_all(
+            sent.reshape(groups * columns, -1), ("group", "col"), 0, 0, tiled=True
+        ).reshape(groups, columns, -1)
+        me = lax.axis_index("group")
+        order = [(me + by) % groups for by in (0, 3, 1, 2)]
+        got = [lax.dynamic_index_in_dim(got, g, 0, False) for g in order]
+        got = [got[0], jnp.concatenate(got[1:3]), got[3]]
+        rows = [g[:, :tok] for g in got]
+        maps = [g[:, tok:].reshape(-1, NGRAM, tok) for g in got]
+        counts = [jnp.sum((r < R_GRP).astype(jnp.int32), axis=1) for r in rows]
+        return rows, maps, counts
+
+    grads, plan = token_grads(
+        keyvalue_cotangent,
+        keyvalue_weight,
+        layer_input,
+        residual_cotangent,
+        norm_gain,
+        lanes,
+        slots_of(ngram_ids, groups),
     )
     planes = [[q * 2 + core for q in range(columns // 2)] for core in range(2)]
     own = lax.all_to_all(
@@ -350,11 +365,14 @@
         tiled=True,
     ).reshape(columns, tok, lanes)
     half = columns // 2
-    left, right = ring(own, 1), ring(own, 3)
+    low, high = own[:half], own[half:]
+    low_left, high_right = ring(low, 1), ring(high, 3)
+    high_left, low_right = ring(high, 1), ring(low, 3)
+    rows, maps, counts = exchange(lax.optimization_barrier((plan, low, high))[0])
     grad = scattered((own,), maps[0], rows[0], counts[0], None)
-    left, right, grad = lax.optimization_barrier((left, right, grad))
-    far = (ring(left[:half], 1), ring(right[half:], 3))
-    grad = scattered((left, right), maps[1], rows[1], counts[1], grad)
+    far = (ring(low_left, 1), ring(high_right, 3))
+    near = (low_left, high_left, low_right, high_right)
+    grad = scattered(near, maps[1], rows[1], counts[1], grad)
     grad = scattered(far, maps[2], rows[2], counts[2], grad)[:R_GRP]
     partial = jnp.sum(grad * grad, axis=1).reshape(-1, lanes)
     squares = col_sum(partial) / width

time: 195 us -> 183 us (0.938)
  the two profiles are of different devices: /device:TPU:22 before, /device:TPU:14 now
where the time goes in v5:
time: 183 us; the launch traced here: 182 us
  starting transfers between devices  49.4 us (27%)
  Pallas kernels  47 us (26%)
  waiting for transfers between devices  40 us (22%)
  blocking collectives  21.8 us (12%)
  local copies, waits for them, and re-layouts  15.2 us (8%)
  other arithmetic  7.46 us (4%)
    ppermute x31, waiting for transfers between devices, shifted(): return lax.ppermute(value, 'col', pairs)  36.1 us
    ppermute x31, starting transfers between devices, shifted(): return lax.ppermute(value, 'col', pairs)  35 us
    pallas_call x3, Pallas kernels, scattered(): pl.pallas_call(functools.partial(scatter_kernel, held is None, parts, per...  33.2 us
    all_to_all x1, blocking collectives, shards(): lax.all_to_all(grads.reshape(columns // 2, 2 * tok, lanes), 'col', 0, 0,...  21.8 us
    unnamed x34, local copies, waits for them, and re-layouts  9.26 us
    all_to_all x1, starting transfers between devices, exchange(): lax.all_to_all(sent.reshape(groups * columns, -1), ('group', 'col'), 0, 0...  7.87 us
    pallas_call x1, Pallas kernels, token_grads(): vmem_call(functools.partial(product_kernel, pieces, True, False, columns)...  7.33 us
    ppermute x6, starting transfers between devices, ring(): return lax.ppermute(x, 'group', [(d, (d + by) % n) for d in range(n)])  6.49 us
  transfers between devices with their start and end apart: 38, of which 18 were waited for; matrix products, arithmetic and copies ran while one was open for 4% of the time, Pallas kernels for 19%

profile of v5, /device:TPU:14, one launch (start us, length us, event | category | flops | bytes accessed | tf_op | source)
XLA Modules:
  0.0 182.1 jit_solution(8061006038953740112)
XLA Ops:
  1.8 2.0 %collective-permute-start.9 = (bf16[128,1024]{1,0:T(8,128)(2,1)S(1)}, bf16[128,1024]{1,0:T(8,128)(2,1)S(1)}, u32[]{:S(2)}, u32[]{:S(2)}) collective-permute-start(bf16[128,1024]{1,0:T(8,128)(2,1)S(1)} %get-tuple-element.22), channel_id=1, source_target_pairs={{0,8},{1,9},{2,10},{3,11},{4,12},{5,13},{6,14},{7,15},{8,16},{9,17... | collective-permute-start | bytes 786440 | tf_op jit(solution)/shard_map/ppermute | solution.py:127
  3.8 2.2 %collective-permute-start.13 = (bf16[128,1024]{1,0:T(8,128)(2,1)S(1)}, bf16[128,1024]{1,0:T(8,128)(2,1)S(1)}, u32[]{:S(2)}, u32[]{:S(2)}) collective-permute-start(bf16[128,1024]{1,0:T(8,128)(2,1)S(1)} %get-tuple-element.22), channel_id=1, source_target_pairs={{0,24},{1,25},{2,26},{3,27},{4,28},{5,29},{6,30},{7,31},{8,0},{9,1... | collective-permute-start | bytes 786440 | tf_op jit(solution)/shard_map/ppermute | solution.py:127
  9.2 3.1 %collective-permute-done.9 = bf16[128,1024]{1,0:T(8,128)(2,1)S(1)} collective-permute-done((bf16[128,1024]{1,0:T(8,128)(2,1)S(1)}, bf16[128,1024]{1,0:T(8,128)(2,1)S(1)}, u32[]{:S(2)}, u32[]{:S(2)}) %collective-permute-start.9) | collective-permute-done | bytes 262176 | tf_op jit(solution)/shard_map/ppermute | solution.py:127
  13.8 2.8 %collective-permute-start.14 = (bf16[64,1024]{1,0:T(8,128)(2,1)S(1)}, bf16[64,1024]{1,0:T(8,128)(2,1)S(1)}, u32[]{:S(2)}, u32[]{:S(2)}) collective-permute-start(bf16[64,1024]{1,0:T(8,128)(2,1)S(1)} %slice.81), channel_id=1, source_target_pairs={{0,24},{1,25},{2,26},{3,27},{4,28},{5,29},{6,30},{7,31},{8,0},{9,1... | collective-permute-start | bytes 393224 | tf_op jit(solution)/shard_map/ppermute | solution.py:127
  20.1 8.3 %collective-permute-done.4 = bf16[64,1024]{1,0:T(8,128)(2,1)S(1)} collective-permute-done((bf16[64,1024]{1,0:T(8,128)(2,1)S(1)}, bf16[64,1024]{1,0:T(8,128)(2,1)S(1)}, u32[]{:S(2)}, u32[]{:S(2)}) %collective-permute-start.4) | collective-permute-done | bytes 131104 | tf_op jit(solution)/shard_map/ppermute | solution.py:127
  29.3 2.3 %collective-permute-start.18 = (bf16[256,1024]{1,0:T(8,128)(2,1)S(1)}, bf16[256,1024]{1,0:T(8,128)(2,1)S(1)}, u32[]{:S(2)}, u32[]{:S(2)}) collective-permute-start(bf16[256,1024]{1,0:T(8,128)(2,1)S(1)} %pad_maximum_fusion.refs_3_), channel_id=1, source_target_pairs={{0,24},{1,25},{2,26},{3,27},{4,28},{5,29},{6,30},{7,31},{8,0},{9,1... | collective-permute-start | bytes 1572872 | tf_op jit(solution)/shard_map/ppermute | solution.py:127
  37.4 4.5 %collective-permute-done.2.refs_5_ = bf16[256,1024]{1,0:T(8,128)(2,1)S(1)} collective-permute-done((bf16[256,1024]{1,0:T(8,128)(2,1)S(1)}, bf16[256,1024]{1,0:T(8,128)(2,1)S(1)}, u32[]{:S(2)}, u32[]{:S(2)}) %collective-permute-start.2) | collective-permute-done | bytes 524320 | tf_op jit(solution)/shard_map/ppermute | solution.py:127
  45.4 2.3 %collective-permute-done.20.refs_13_ = bf16[256,1024]{1,0:T(8,128)(2,1)S(1)} collective-permute-done((bf16[256,1024]{1,0:T(8,128)(2,1)S(1)}, bf16[256,1024]{1,0:T(8,128)(2,1)S(1)}, u32[]{:S(2)}, u32[]{:S(2)}) %collective-permute-start.20) | collective-permute-done | bytes 524320 | tf_op jit(solution)/shard_map/ppermute | solution.py:127
  49.0 6.9 %collective-permute-done.15.refs_14_ = bf16[256,1024]{1,0:T(8,128)(2,1)} collective-permute-done((bf16[256,1024]{1,0:T(8,128)(2,1)}, bf16[256,1024]{1,0:T(8,128)(2,1)}, u32[]{:S(2)}, u32[]{:S(2)}) %collective-permute-start.15) | collective-permute-done | bytes 524320 | tf_op jit(solution)/shard_map/ppermute | solution.py:127
  58.6 3.2 %collective-permute-start.8 = (bf16[256,1024]{1,0:T(8,128)(2,1)}, bf16[256,1024]{1,0:T(8,128)(2,1)}, u32[]{:S(2)}, u32[]{:S(2)}) collective-permute-start(bf16[256,1024]{1,0:T(8,128)(2,1)} %collective-permute-done.7.refs_8_), channel_id=1, source_target_pairs={{0,24},{1,25},{2,26},{3,27},{4,28},{5,29},{6,30},{7,31},{8,0},{9,1... | collective-permute-start | bytes 1572872 | tf_op jit(solution)/shard_map/ppermute | solution.py:127
  66.0 7.3 %product_near.1 = (f32[16,2,128,128]{3,2,1,0:T(8,128)S(1)}, f32[2,128,128]{2,1,0:T(8,128)S(1)}) custom-call(s32[16]{0:T(128)S(1)} %stack.67.refs_0_.where, bf16[128,2048]{1,0:T(8,128)(2,1)S(1)} %copy-done.1, bf16[128,2048]{1,0:T(8,128)(2,1)} %collective-permute-done.refs_2_, bf16[256,1024]{1,0:T(8,128)(2,1)S(1)} %pad_maximum_fusion.refs_3_, ...), custom_call_target="tpu_custom_call" | custom-call | tf_op jit(solution)/shard_map/product_near/pallas_call | solution.py:184
  73.4 4.0 %product_far.1 = (f32[16,2,128,128]{3,2,1,0:T(8,128)S(1)}, f32[2,128,128]{2,1,0:T(8,128)S(1)}) custom-call(s32[16]{0:T(128)S(1)} %stack.67.refs_0_.where, bf16[128,2048]{1,0:T(8,128)(2,1)S(1)} %copy-done.1, bf16[128,2048]{1,0:T(8,128)(2,1)} %collective-permute-done.refs_2_, ...), custom_call_target="tpu_custom_call", output_to_operand_aliasing={{0}: (7, {})} | custom-call | tf_op jit(solution)/shard_map/product_far/pallas_call | solution.py:196
  78.9 2.4 %token_grads.1 = bf16[16,2,128,128]{3,2,1,0:T(8,128)(2,1)S(1)} custom-call(s32[16]{0:T(128)S(1)} %stack.67.refs_0_.where, f32[16,2,128,128]{3,2,1,0:T(8,128)S(1)} %get-tuple-element.12.ng, f32[2,128,128]{2,1,0:T(8,128)S(1)} %get-tuple-element.13.ss, f32[2,128,128]{2,1,0:T(8,128)S(1)} %get-tuple-element.14.inner, ...), custom_call_target="tpu_custom_call" | custom-call | tf_op jit(solution)/shard_map/token_grads/pallas_call | solution.py:205
  81.3 21.8 %all_to_all.14 = bf16[16,256,128]{2,1,0:T(8,128)(2,1)S(1)} all-to-all(bf16[16,256,128]{2,1,0:T(8,128)(2,1)S(1)} %bitcast.48), channel_id=1, replica_groups={{0,2,4,6,8,10,12,14,16,18,20,22,24,26,28,30},{1,3,5,7,9,11,13,15,17,19,..., dimensions={0} | all-to-all | bytes 2097152 | tf_op jit(solution)/shard_map/all_to_all | solution.py:359
  107.0 7.9 %all-to-all-start.1 = ((s32[128,1,384]{2,1,0:T(1,128)}), s32[128,1,384]{2,1,0:T(1,128)S(1)}, u32[]{:S(2)}, u32[]{:S(2)}) async-start(s32[128,1,384]{2,1,0:T(1,128)} %all_to_all.10), calls=%async_computation.1 | async-start | bytes 393216 | tf_op jit(solution)/shard_map/all_to_all | solution.py:337
  120.4 2.6 %all-to-all-done.1 = s32[128,1,384]{2,1,0:T(1,128)S(1)} async-done(((s32[128,1,384]{2,1,0:T(1,128)}), s32[128,1,384]{2,1,0:T(1,128)S(1)}, u32[]{:S(2)}, u32[]{:S(2)}) %all-to-all-start.1) | async-done | bytes 196640 | tf_op jit(solution)/shard_map/all_to_all | solution.py:337
  123.3 7.8 %scatter_rows.3.refs_5_ = f32[8200,128]{1,0:T(8,128)S(1)} custom-call(s32[4096]{0:T(1024)S(1)} %get-tuple-element.31.rows, s32[32]{0:T(128)S(1)} %get-tuple-element.30.counts, bf16[32,128,128]{2,1,0:T(8,128)(2,1)S(1)} %bitcast.47, s32[32,2,128]{2,1,0:T(2,128)S(1)} %reshape.173.refs_1_), custom_call_target="tpu_custom_call" | custom-call | flops 1000000 | bytes 28800000 | tf_op jit(solution)/shard_map/scatter_rows/pallas_call | solution.py:288
  131.6 16.3 %scatter_rows.4.refs_3_ = f32[8200,128]{1,0:T(8,128)S(1)} custom-call(s32[8192]{0:T(1024)S(1)} %get-tuple-element.29.rows, s32[64]{0:T(128)S(1)} %get-tuple-element.28.counts, bf16[16,128,128]{2,1,0:T(8,128)(2,1)S(1)} %collective-permute-done.24.refs_0_, bf16[16,128,128]{2,1,0:T(8,128)(2,1)} %collective-permute-done.28.refs_1_, ...), custom_call_target="tpu_custom_call", output_to_operand_aliasing={{}: (7, {})} | custom-call | flops 1000000 | bytes 57600000 | tf_op jit(solution)/shard_map/scatter_rows/pallas_call | solution.py:288
  147.9 9.0 %scatter_rows.5 = f32[8200,128]{1,0:T(8,128)S(1)} custom-call(s32[4096]{0:T(1024)S(1)} %get-tuple-element.33.rows, s32[32]{0:T(128)S(1)} %get-tuple-element.32.counts, bf16[16,128,128]{2,1,0:T(8,128)(2,1)S(1)} %collective-permute-done.25.refs_0_, bf16[16,128,128]{2,1,0:T(8,128)(2,1)} %collective-permute-done.27.refs_1_, ...), custom_call_target="tpu_custom_call", output_to_operand_aliasing={{}: (5, {})} | custom-call | flops 1000000 | bytes 28800000 | tf_op jit(solution)/shard_map/scatter_rows/pallas_call | solution.py:288
  159.7 4.4 %collective-permute-start.31 = (f32[64,128]{1,0:T(8,128)S(1)}, f32[64,128]{1,0:T(8,128)S(1)}, u32[]{:S(2)}, u32[]{:S(2)}) collective-permute-start(f32[64,128]{1,0:T(8,128)S(1)} %bitcast_add_fusion.1), channel_id=1, source_target_pairs={{0,4},{1,5},{2,6},{3,7},{4,0},{5,1},{6,2},{7,3},{8,12},{9,13},{10,... | collective-permute-start | bytes 98312 | tf_op jit(solution)/shard_map/ppermute | solution.py:127
  166.2 1.9 %collective-permute-done.32 = f32[64,128]{1,0:T(8,128)S(1)} collective-permute-done((f32[64,128]{1,0:T(8,128)S(1)}, f32[64,128]{1,0:T(8,128)S(1)}, u32[]{:S(2)}, u32[]{:S(2)}) %collective-permute-start.32) | collective-permute-done | bytes 32800 | tf_op jit(solution)/shard_map/ppermute | solution.py:127
  168.0 2.9 %collective-permute-done.33 = f32[64,128]{1,0:T(8,128)S(1)} collective-permute-done((f32[64,128]{1,0:T(8,128)S(1)}, f32[64,128]{1,0:T(8,128)S(1)}, u32[]{:S(2)}, u32[]{:S(2)}) %collective-permute-start.33) | collective-permute-done | bytes 32800 | tf_op jit(solution)/shard_map/ppermute | solution.py:127
  172.5 2.4 %collective-permute-start.36 = (f32[64,128]{1,0:T(8,128)S(1)}, f32[64,128]{1,0:T(8,128)S(1)}, u32[]{:S(2)}, u32[]{:S(2)}) collective-permute-start(f32[64,128]{1,0:T(8,128)S(1)} %add_add_fusion), channel_id=1, source_target_pairs={{0,24},{1,25},{2,26},{3,27},{4,28},{5,29},{6,30},{7,31},{8,0},{9,1... | collective-permute-start | bytes 98312 | tf_op jit(solution)/shard_map/ppermute | solution.py:127
  177.5 4.7 %multiply_subtract_fusion = f32[8192,128]{1,0:T(8,128)} fusion(f32[8192,128]{1,0:T(8,128)S(1)} %copy-done.9, f32[8200,128]{1,0:T(8,128)S(1)} %scatter_rows.5, f32[8192]{0:T(1024)S(1)} %get-tuple-element.16), kind=kLoop, calls=%fused_computation | loop fusion | flops 2097152 | bytes 12615680 | tf_op jit(solution)/shard_map/sub | solution.py:380
  (135 shorter events, 48.0 us)
Async XLA Ops:
  1.8 10.4 %collective-permute-start.9 = (bf16[128,1024]{1,0:T(8,128)(2,1)S(1)}, bf16[128,1024]{1,0:T(8,128)(2,1)S(1)}, u32[]{:S(2)}, u32[]{:S(2)}) collective-permute-start(bf16[128,1024]{1,0:T(8,128)(2,1)S(1)} %get-tuple-element.22), channel_id=1, source_target_pairs={{0,8},{1,9},{2,10},{3,11},{4,12},{5,13},{6,14},{7,15},{8,16},{9,17... | collective-permute-start | bytes 786440 | tf_op jit(solution)/shard_map/ppermute | solution.py:127
  8.0 23.6 %collective-permute-start = (bf16[128,2048]{1,0:T(8,128)(2,1)}, bf16[128,2048]{1,0:T(8,128)(2,1)}, u32[]{:S(2)}, u32[]{:S(2)}) collective-permute-start(bf16[128,2048]{1,0:T(8,128)(2,1)} %refs_1_.1), channel_id=1, source_target_pairs={{0,1},{1,0},{2,3},{3,2},{4,5},{5,4},{6,7},{7,6},{8,9},{9,8},{10,11... | collective-permute-start | bytes 1572872 | tf_op jit(solution)/shard_map/ppermute | solution.py:127
  12.4 22.4 %collective-permute-start.10 = (bf16[256,1024]{1,0:T(8,128)(2,1)S(1)}, bf16[256,1024]{1,0:T(8,128)(2,1)}, u32[]{:S(2)}, u32[]{:S(2)}) collective-permute-start(bf16[256,1024]{1,0:T(8,128)(2,1)S(1)} %pad_maximum_fusion.1.refs_9_), channel_id=1, source_target_pairs={{0,2},{1,3},{2,4},{3,5},{4,6},{5,7},{6,0},{7,1},{8,10},{9,11},{10,... | collective-permute-start | bytes 1572872 | tf_op jit(solution)/shard_map/ppermute | solution.py:127
  16.6 11.8 %collective-permute-start.4 = (bf16[64,1024]{1,0:T(8,128)(2,1)S(1)}, bf16[64,1024]{1,0:T(8,128)(2,1)S(1)}, u32[]{:S(2)}, u32[]{:S(2)}) collective-permute-start(bf16[64,1024]{1,0:T(8,128)(2,1)S(1)} %slice.78), channel_id=1, source_target_pairs={{0,2},{1,3},{2,4},{3,5},{4,6},{5,7},{6,0},{7,1},{8,10},{9,11},{10,... | collective-permute-start | bytes 393224 | tf_op jit(solution)/shard_map/ppermute | solution.py:127
  18.5 10.8 %collective-permute-start.6 = (bf16[64,1024]{1,0:T(8,128)(2,1)S(1)}, bf16[64,1024]{1,0:T(8,128)(2,1)S(1)}, u32[]{:S(2)}, u32[]{:S(2)}) collective-permute-start(bf16[64,1024]{1,0:T(8,128)(2,1)S(1)} %slice.79), channel_id=1, source_target_pairs={{0,6},{1,7},{2,0},{3,1},{4,2},{5,3},{6,4},{7,5},{8,14},{9,15},{10,... | collective-permute-start | bytes 393224 | tf_op jit(solution)/shard_map/ppermute | solution.py:127
  20.0 38.5 %collective-permute-start.21 = (bf16[128,4096]{1,0:T(8,128)(2,1)S(1)}, bf16[128,4096]{1,0:T(8,128)(2,1)S(1)}, u32[]{:S(2)}, u32[]{:S(2)}) collective-permute-start(bf16[128,4096]{1,0:T(8,128)(2,1)S(1)} %copy-done), channel_id=1, source_target_pairs={{0,1},{1,0},{2,3},{3,2},{4,5},{5,4},{6,7},{7,6},{8,9},{9,8},{10,11... | collective-permute-start | bytes 3145736 | tf_op jit(solution)/shard_map/ppermute | solution.py:127
  28.4 13.5 %collective-permute-start.2 = (bf16[256,1024]{1,0:T(8,128)(2,1)S(1)}, bf16[256,1024]{1,0:T(8,128)(2,1)S(1)}, u32[]{:S(2)}, u32[]{:S(2)}) collective-permute-start(bf16[256,1024]{1,0:T(8,128)(2,1)S(1)} %pad_maximum_fusion.refs_3_), channel_id=1, source_target_pairs={{0,8},{1,9},{2,10},{3,11},{4,12},{5,13},{6,14},{7,15},{8,16},{9,17... | collective-permute-start | bytes 1572872 | tf_op jit(solution)/shard_map/ppermute | solution.py:127
  29.3 14.0 %collective-permute-start.18 = (bf16[256,1024]{1,0:T(8,128)(2,1)S(1)}, bf16[256,1024]{1,0:T(8,128)(2,1)S(1)}, u32[]{:S(2)}, u32[]{:S(2)}) collective-permute-start(bf16[256,1024]{1,0:T(8,128)(2,1)S(1)} %pad_maximum_fusion.refs_3_), channel_id=1, source_target_pairs={{0,24},{1,25},{2,26},{3,27},{4,28},{5,29},{6,30},{7,31},{8,0},{9,1... | collective-permute-start | bytes 1572872 | tf_op jit(solution)/shard_map/ppermute | solution.py:127
  31.6 16.1 %collective-permute-start.20 = (bf16[256,1024]{1,0:T(8,128)(2,1)S(1)}, bf16[256,1024]{1,0:T(8,128)(2,1)S(1)}, u32[]{:S(2)}, u32[]{:S(2)}) collective-permute-start(bf16[256,1024]{1,0:T(8,128)(2,1)S(1)} %pad_maximum_fusion.1.refs_9_), channel_id=1, source_target_pairs={{0,6},{1,7},{2,0},{3,1},{4,2},{5,3},{6,4},{7,5},{8,14},{9,15},{10,... | collective-permute-start | bytes 1572872 | tf_op jit(solution)/shard_map/ppermute | solution.py:127
  34.8 21.1 %collective-permute-start.15 = (bf16[256,1024]{1,0:T(8,128)(2,1)}, bf16[256,1024]{1,0:T(8,128)(2,1)}, u32[]{:S(2)}, u32[]{:S(2)}) collective-permute-start(bf16[256,1024]{1,0:T(8,128)(2,1)} %constant_dynamic-update-slice_fusion.3.refs_10_), channel_id=1, source_target_pairs={{0,6},{1,7},{2,0},{3,1},{4,2},{5,3},{6,4},{7,5},{8,14},{9,15},{10,... | collective-permute-start | bytes 1572872 | tf_op jit(solution)/shard_map/ppermute | solution.py:127
  41.9 14.5 %collective-permute-start.7 = (bf16[256,1024]{1,0:T(8,128)(2,1)}, bf16[256,1024]{1,0:T(8,128)(2,1)}, u32[]{:S(2)}, u32[]{:S(2)}) collective-permute-start(bf16[256,1024]{1,0:T(8,128)(2,1)} %constant_dynamic-update-slice_fusion.refs_4_), channel_id=1, source_target_pairs={{0,24},{1,25},{2,26},{3,27},{4,28},{5,29},{6,30},{7,31},{8,0},{9,1... | collective-permute-start | bytes 1572872 | tf_op jit(solution)/shard_map/ppermute | solution.py:127
  44.1 12.8 %collective-permute-start.17 = (bf16[256,1024]{1,0:T(8,128)(2,1)}, bf16[256,1024]{1,0:T(8,128)(2,1)}, u32[]{:S(2)}, u32[]{:S(2)}) collective-permute-start(bf16[256,1024]{1,0:T(8,128)(2,1)} %constant_dynamic-update-slice_fusion.refs_4_), channel_id=1, source_target_pairs={{0,8},{1,9},{2,10},{3,11},{4,12},{5,13},{6,14},{7,15},{8,16},{9,17... | collective-permute-start | bytes 1572872 | tf_op jit(solution)/shard_map/ppermute | solution.py:127
  55.9 21.6 %collective-permute-start.23 = (bf16[128,4096]{1,0:T(8,128)(2,1)}, bf16[128,4096]{1,0:T(8,128)(2,1)}, u32[]{:S(2)}, u32[]{:S(2)}) collective-permute-start(bf16[128,4096]{1,0:T(8,128)(2,1)} %r_own.1), channel_id=1, source_target_pairs={{0,1},{1,0},{2,3},{3,2},{4,5},{5,4},{6,7},{7,6},{8,9},{9,8},{10,11... | collective-permute-start | bytes 3145736 | tf_op jit(solution)/shard_map/ppermute | solution.py:127
  56.4 17.0 %collective-permute-start.11 = (bf16[256,1024]{1,0:T(8,128)(2,1)}, bf16[256,1024]{1,0:T(8,128)(2,1)}, u32[]{:S(2)}, u32[]{:S(2)}) collective-permute-start(bf16[256,1024]{1,0:T(8,128)(2,1)} %collective-permute-done.10.refs_11_), channel_id=1, source_target_pairs={{0,2},{1,3},{2,4},{3,5},{4,6},{5,7},{6,0},{7,1},{8,10},{9,11},{10,... | collective-permute-start | bytes 1572872 | tf_op jit(solution)/shard_map/ppermute | solution.py:127
  56.9 16.5 %collective-permute-start.3 = (bf16[256,1024]{1,0:T(8,128)(2,1)}, bf16[256,1024]{1,0:T(8,128)(2,1)}, u32[]{:S(2)}, u32[]{:S(2)}) collective-permute-start(bf16[256,1024]{1,0:T(8,128)(2,1)} %copy-done.3), channel_id=1, source_target_pairs={{0,8},{1,9},{2,10},{3,11},{4,12},{5,13},{6,14},{7,15},{8,16},{9,17... | collective-permute-start | bytes 1572872 | tf_op jit(solution)/shard_map/ppermute | solution.py:127
  58.0 15.4 %collective-permute-start.16 = (bf16[256,1024]{1,0:T(8,128)(2,1)}, bf16[256,1024]{1,0:T(8,128)(2,1)}, u32[]{:S(2)}, u32[]{:S(2)}) collective-permute-start(bf16[256,1024]{1,0:T(8,128)(2,1)} %collective-permute-done.15.refs_14_), channel_id=1, source_target_pairs={{0,6},{1,7},{2,0},{3,1},{4,2},{5,3},{6,4},{7,5},{8,14},{9,15},{10,... | collective-permute-start | bytes 1572872 | tf_op jit(solution)/shard_map/ppermute | solution.py:127
  58.6 14.9 %collective-permute-start.8 = (bf16[256,1024]{1,0:T(8,128)(2,1)}, bf16[256,1024]{1,0:T(8,128)(2,1)}, u32[]{:S(2)}, u32[]{:S(2)}) collective-permute-start(bf16[256,1024]{1,0:T(8,128)(2,1)} %collective-permute-done.7.refs_8_), channel_id=1, source_target_pairs={{0,24},{1,25},{2,26},{3,27},{4,28},{5,29},{6,30},{7,31},{8,0},{9,1... | collective-permute-start | bytes 1572872 | tf_op jit(solution)/shard_map/ppermute | solution.py:127
  104.0 13.7 %collective-permute-start.24 = (bf16[16,128,128]{2,1,0:T(8,128)(2,1)S(1)}, bf16[16,128,128]{2,1,0:T(8,128)(2,1)S(1)}, u32[]{:S(2)}, u32[]{:S(2)}) collective-permute-start(bf16[16,128,128]{2,1,0:T(8,128)(2,1)S(1)} %bitcast.50), channel_id=1, source_target_pairs={{0,32},{32,64},{64,96},{96,0},{1,33},{33,65},{65,97},{97,1},{2,34}... | collective-permute-start | bytes 1572872 | tf_op jit(solution)/shard_map/ppermute | solution.py:311
  105.6 14.2 %collective-permute-start.26 = (bf16[16,128,128]{2,1,0:T(8,128)(2,1)}, bf16[16,128,128]{2,1,0:T(8,128)(2,1)S(1)}, u32[]{:S(2)}, u32[]{:S(2)}) collective-permute-start(bf16[16,128,128]{2,1,0:T(8,128)(2,1)} %bitcast.21), channel_id=1, source_target_pairs={{0,96},{32,0},{64,32},{96,64},{1,97},{33,1},{65,33},{97,65},{2,98}... | collective-permute-start | bytes 1572872 | tf_op jit(solution)/shard_map/ppermute | solution.py:311
  107.0 16.1 %all-to-all-start.1 = ((s32[128,1,384]{2,1,0:T(1,128)}), s32[128,1,384]{2,1,0:T(1,128)S(1)}, u32[]{:S(2)}, u32[]{:S(2)}) async-start(s32[128,1,384]{2,1,0:T(1,128)} %all_to_all.10), calls=%async_computation.1 | async-start | bytes 393216 | tf_op jit(solution)/shard_map/all_to_all | solution.py:337
  114.8 16.5 %collective-permute-start.28 = (bf16[16,128,128]{2,1,0:T(8,128)(2,1)}, bf16[16,128,128]{2,1,0:T(8,128)(2,1)}, u32[]{:S(2)}, u32[]{:S(2)}) collective-permute-start(bf16[16,128,128]{2,1,0:T(8,128)(2,1)} %bitcast.21), channel_id=1, source_target_pairs={{0,32},{32,64},{64,96},{96,0},{1,33},{33,65},{65,97},{97,1},{2,34}... | collective-permute-start | bytes 1572872 | tf_op jit(solution)/shard_map/ppermute | solution.py:311
  116.4 15.2 %collective-permute-start.29 = (bf16[16,128,128]{2,1,0:T(8,128)(2,1)S(1)}, bf16[16,128,128]{2,1,0:T(8,128)(2,1)}, u32[]{:S(2)}, u32[]{:S(2)}) collective-permute-start(bf16[16,128,128]{2,1,0:T(8,128)(2,1)S(1)} %bitcast.51), channel_id=1, source_target_pairs={{0,96},{32,0},{64,32},{96,64},{1,97},{33,1},{65,33},{97,65},{2,98}... | collective-permute-start | bytes 1572872 | tf_op jit(solution)/shard_map/ppermute | solution.py:311
  117.8 30.1 %collective-permute-start.25 = (bf16[16,128,128]{2,1,0:T(8,128)(2,1)S(1)}, bf16[16,128,128]{2,1,0:T(8,128)(2,1)S(1)}, u32[]{:S(2)}, u32[]{:S(2)}) collective-permute-start(bf16[16,128,128]{2,1,0:T(8,128)(2,1)S(1)} %collective-permute-done.24.refs_0_), channel_id=1, source_target_pairs={{0,32},{32,64},{64,96},{96,0},{1,33},{33,65},{65,97},{97,1},{2,34}... | collective-permute-start | bytes 1572872 | tf_op jit(solution)/shard_map/ppermute | solution.py:311
  119.8 28.1 %collective-permute-start.27 = (bf16[16,128,128]{2,1,0:T(8,128)(2,1)S(1)}, bf16[16,128,128]{2,1,0:T(8,128)(2,1)}, u32[]{:S(2)}, u32[]{:S(2)}) collective-permute-start(bf16[16,128,128]{2,1,0:T(8,128)(2,1)S(1)} %collective-permute-done.26.refs_3_), channel_id=1, source_target_pairs={{0,96},{32,0},{64,32},{96,64},{1,97},{33,1},{65,33},{97,65},{2,98}... | collective-permute-start | bytes 1572872 | tf_op jit(solution)/shard_map/ppermute | solution.py:311
  (28 other events, 283.1 us)
